TPU v7x, 512 devices: a whole 4x4x16 slice. The times are simulated.
512 devices in a mesh: dp: 64 (over x_lo, z, core), fsdp: 8 (over y, x_hi).
Axes of the slice: x: 4 (x_hi: 2, x_lo: 2; x = x_hi * 2 + x_lo), y: 4, z: 16, core: 2. Of those that a mesh axis runs over, the one named last changes fastest.
Arguments:
- tokens: bfloat16 [65536, 1024], P('dp'), may hold values from -8 to 8
- teacher: bfloat16 [512, 6144], P('dp'), may hold values from -8 to 8
- norm_gain: float32 [1024], replicated, may hold values from 0.25 to 1.75
- w_in: bfloat16 [1024, 4096], P(None, 'fsdp'), may hold values from -0.1875 to 0.1875
- b_in: float32 [4096], P('fsdp'), may hold values from -3 to 3
- w_out: bfloat16 [1024, 4096], P(None, 'fsdp'), may hold values from -0.09375 to 0.09375
- b_out: float32 [1024], replicated, may hold values from -3 to 3
- final_gain: float32 [1024], replicated, may hold values from 0.25 to 1.75
Outputs:
- loss_value: float32 [], replicated
- grad_in: bfloat16 [1024, 4096], P('dp', 'fsdp')
- grad_out: bfloat16 [1024, 4096], P('dp', 'fsdp')
All inputs are finite; a program needn't handle non-finite values.
Results may differ from a plain program's by a relative error of at most 0.008.
Values may be sent and summed in bfloat16 or wider, within the bound.
A program may use at most 64 MiB of HBM per device.

v0:
```python
import jax
import jax.numpy as jnp
from jax import lax
from jax.sharding import PartitionSpec as P

loss_scale = 4096.0


def gelu_tanh(values):
    inner = 0.7978845608 * (values + 0.044715 * values * values * values)
    return 0.5 * values * (1.0 + jnp.tanh(inner))


def gelu_slope(values):
    inner = 0.7978845608 * (values + 0.044715 * values * values * values)
    tangent = jnp.tanh(inner)
    return 0.5 * (1.0 + tangent) + 0.5 * values * (1.0 - tangent * tangent) * 0.7978845608 * (
        1.0 + 3.0 * 0.044715 * values * values
    )


def layer_norm(values, gain_vec):
    centered = values - jnp.mean(values, axis=-1, keepdims=True)
    inv_std = lax.rsqrt(jnp.mean(centered * centered, axis=-1, keepdims=True) + 1e-05)
    normed = centered * inv_std
    return (normed * gain_vec, normed, inv_std)


def contract_last(left_side, right_side):
    return lax.dot_general(
        left_side, right_side, (((1,), (1,)), ((), ())), preferred_element_type=jnp.float32
    )


def contract_first(left_side, right_side):
    return lax.dot_general(
        left_side, right_side, (((0,), (0,)), ((), ())), preferred_element_type=jnp.float32
    )


def body(tokens, teacher, norm_gain, w_in, b_in, w_out, b_out, final_gain):
    dp_size = lax.axis_size("dp")
    fsdp_size = lax.axis_size("fsdp")
    block_rows = teacher.shape[0]
    model_width = tokens.shape[1]
    per_image = tokens.shape[0] // block_rows
    image_count = block_rows * dp_size
    token_values = tokens.astype(jnp.float32)
    normed_tokens = layer_norm(token_values, norm_gain)[0].astype(jnp.bfloat16)
    pre_act = jnp.dot(normed_tokens, w_in, preferred_element_type=jnp.float32) + b_in
    hidden = pre_act.shape[1]
    pooled = (
        gelu_tanh(pre_act).reshape(block_rows, per_image, hidden).mean(axis=1).astype(jnp.bfloat16)
    )
    token_mean = token_values.reshape(block_rows, per_image, model_width).mean(axis=1)
    partial_value = contract_last(pooled, w_out)
    embedding = token_mean + lax.psum(partial_value, "fsdp") + b_out
    scaled_unit, normed_embed, inv_std = layer_norm(embedding, final_gain)
    unit_norm = jnp.sqrt(jnp.sum(scaled_unit * scaled_unit, axis=-1, keepdims=True) + 1e-06)
    unit_dir = scaled_unit / unit_norm
    student = unit_dir.astype(jnp.bfloat16)
    teacher_f = teacher.astype(jnp.float32)
    target = (
        teacher_f / jnp.sqrt(jnp.sum(teacher_f * teacher_f, axis=-1, keepdims=True) + 1e-06)
    ).astype(jnp.bfloat16)
    rows_each = block_rows // fsdp_size
    first_row = lax.axis_index("fsdp") * rows_each
    own_student = lax.dynamic_slice_in_dim(student, first_row, rows_each, 0)
    own_target = lax.dynamic_slice_in_dim(target, first_row, rows_each, 0)
    piece_student = lax.all_gather(student, "dp", axis=0, tiled=True)
    piece_target = lax.all_gather(target, "dp", axis=0, tiled=True)
    resid = contract_last(own_student, piece_student) - contract_last(own_target, piece_target)
    grad_acc = jnp.dot(
        resid.astype(jnp.bfloat16), piece_student, preferred_element_type=jnp.float32
    )
    sum_part = jnp.sum(resid * resid)
    grad_sum = lax.all_gather(grad_acc, "fsdp", axis=0, tiled=True)
    loss_value = lax.psum(sum_part, ("dp", "fsdp")) / image_count
    dstudent = loss_scale * 4.0 / image_count * grad_sum
    dunit = (dstudent - unit_dir * jnp.sum(unit_dir * dstudent, axis=-1, keepdims=True)) / unit_norm
    gain_grad = dunit * final_gain
    dembed = inv_std * (
        gain_grad
        - jnp.mean(gain_grad, axis=-1, keepdims=True)
        - normed_embed * jnp.mean(gain_grad * normed_embed, axis=-1, keepdims=True)
    )
    dembed_b = dembed.astype(jnp.bfloat16)
    dpooled = jnp.dot(dembed_b, w_out, preferred_element_type=jnp.float32)
    slope = gelu_slope(pre_act.reshape(block_rows, per_image, hidden))
    dhidden = (
        (dpooled[:, None, :] / per_image * slope)
        .reshape(block_rows * per_image, hidden)
        .astype(jnp.bfloat16)
    )
    in_term = contract_first(normed_tokens, dhidden)
    out_term = contract_first(dembed_b, pooled)
    shares = lax.psum_scatter(
        jnp.concatenate([in_term, out_term], axis=1), "dp", scatter_dimension=0, tiled=True
    )
    grad_in = shares[:, :hidden].astype(jnp.bfloat16)
    grad_out = shares[:, hidden:].astype(jnp.bfloat16)
    return (loss_value, grad_in, grad_out)


def solution(mesh):
    return jax.shard_map(
        body,
        mesh=mesh,
        in_specs=(
            P("dp", None),
            P("dp", None),
            P(),
            P(None, "fsdp"),
            P("fsdp"),
            P(None, "fsdp"),
            P(),
            P(),
        ),
        out_specs=(P(), P("dp", "fsdp"), P("dp", "fsdp")),
        check_vma=False,
    )
```

profile of v0, /device:TPU:1, one launch (start us, length us, event | category | flops | bytes accessed | tf_op | source)
XLA Modules:
  0.0 591.8 jit_solution(14809419079678232370)
XLA Ops:
  7.2 0.0 copy-start
  7.2 0.0 copy-start.1
  7.2 0.0 all-gather.4.cloned.1.call-start
  7.2 2.1 convert_reduce_fusion
  9.3 0.2 copy-done.1
  9.5 0.0 copy-start.8
  9.5 0.0 copy-start.9
  9.5 0.4 bitcast_reduce_fusion
  9.9 0.7 multiply_reduce_fusion
  10.6 0.0 copy-done
  10.6 0.0 copy-done.8
  10.6 0.0 copy-done.9
  10.6 0.0 copy-start.4
  10.6 0.0 copy-start.7
  10.7 0.0 copy-start.6
  10.7 0.0 copy-start.5
  10.7 3.3 bitcast_reduce_fusion.1
  13.9 0.0 copy-done.4
  13.9 0.4 fusion.16
  14.3 35.8 %psum.14 = f32[8,1024]{1,0:T(8,128)S(1)} all-reduce(f32[8,1024]{1,0:T(8,128)S(1)} %fusion.16), channel_id=1, replica_groups=mesh['dp'=64,'fsdp'=8] {'fsdp'}, use_global_device_ids=true, to_apply=%region_4.0 | all-reduce | flops 8192 | bytes 65536 | tf_op jit(solution)/shard_map/psum | solution.py:57
  50.1 0.0 copy-done.7
  50.1 0.1 fusion.25
  50.2 0.2 multiply_reduce_fusion.4
  50.4 0.0 copy-done.6
  50.4 0.2 multiply_reduce_fusion.3
  50.6 0.7 fusion.21
  51.3 0.0 all-gather.4.cloned.1.call-update
  51.3 0.0 all-gather.6.cloned.1.call-start
  51.4 0.0 copy-done.5
  51.4 0.2 fusion.7
  51.6 0.7 fusion.8
  52.3 0.0 all-gather.6.cloned.1.call-update
  52.3 0.0 reduce-scatter.4.cloned.1.call-start
  52.4 126.7 %all-gather.4.cloned.1.call-done = bf16[512,1024]{1,0:T(8,128)(2,1)} async-done(((bf16[8,1024]{1,0:T(8,128)(2,1)}), bf16[512,1024]{1,0:T(8,128)(2,1)}) %all-gather.4.cloned.1.call-update) | async-done | bytes 1048592 | tf_op jit(solution)/shard_map/all_gather | solution.py:70
  179.1 1.6 fusion.12
  180.7 124.0 %all-gather.6.cloned.1.call-done = bf16[512,6144]{1,0:T(8,128)(2,1)} async-done(((bf16[8,6144]{1,0:T(8,128)(2,1)}), bf16[512,6144]{1,0:T(8,128)(2,1)}) %all-gather.6.cloned.1.call-update) | async-done | bytes 6291472 | tf_op jit(solution)/shard_map/all_gather | solution.py:71
  304.7 0.0 copy-start.2
  304.7 4.6 fusion.9
  309.4 0.6 subtract_convert_fusion
  310.0 0.0 copy-done.2
  310.0 0.2 fusion.27
  310.2 28.0 %all-gather = f32[8192]{0:T(1024)S(1)} all-gather(f32[1024]{0:T(1024)S(1)} %bitcast.24), channel_id=2, replica_groups=mesh['dp'=64,'fsdp'=8] {'fsdp'}, dimensions={0}, use_global_device_ids=true | all-gather | bytes 36864 | tf_op jit(solution)/shard_map/all_gather | solution.py:77
  338.2 0.0 copy-start.3
  338.2 0.2 multiply_reduce_fusion.2
  338.4 0.2 fusion.24
  338.6 1.7 convolution_multiply_fusion
  340.4 0.5 fusion.15
  340.9 0.0 copy-done.3
  340.9 1.4 fusion.6
  342.3 1.5 fusion.22
  343.8 2.5 pad_maximum_fusion
  346.3 5.3 copy.15
  351.6 0.0 reduce-scatter.4.cloned.1.call-update
  351.6 106.5 %psum.15 = f32[]{:T(128)} all-reduce(f32[]{:T(128)} %get-tuple-element.17), channel_id=1, replica_groups=mesh['dp'=64,'fsdp'=8] {'dp','fsdp'}, use_global_device_ids=true, to_apply=%region_10.0 | all-reduce | flops 1 | bytes 8 | tf_op jit(solution)/shard_map/psum | solution.py:78
  458.8 122.9 %reduce-scatter.4.cloned.1.call-done = f32[16,1024]{1,0:T(8,128)} async-done(((f32[1024,1024]{1,0:T(8,128)}), f32[16,1024]{1,0:T(8,128)}) %reduce-scatter.4.cloned.1.call-update) | async-done | bytes 65552
  581.7 1.0 copy.16
  582.7 0.7 copy.14
  583.4 0.7 copy.13
  (11 shorter events, 0.1 us)
Async XLA Ops:
  7.2 3.4 copy-start
  7.2 2.3 copy-start.1
  7.2 171.9 %all-gather.4.cloned.1.call-start = ((), (), s32[]{:S(2)}) async-start(), calls=%async_computation.1 | async-start | bytes 1064960 | tf_op jit(solution)/shard_map/all_gather | solution.py:70
  9.5 1.1 copy-start.8
  9.5 1.1 copy-start.9
  10.6 3.3 copy-start.4
  10.6 39.4 %copy-start.7 = (f32[1024]{0:T(1024)S(1)}, f32[1024]{0:T(1024)}, u32[]{:S(2)}) copy-start(f32[1024]{0:T(1024)} %param.14) | copy-start | bytes 12292
  10.7 39.8 %copy-start.6 = (f32[1024]{0:T(1024)S(1)}, f32[1024]{0:T(1024)}, u32[]{:S(2)}) copy-start(f32[1024]{0:T(1024)} %param.15) | copy-start | bytes 12292
  10.7 40.7 %copy-start.5 = (bf16[8,6144]{1,0:T(8,128)(2,1)S(1)}, bf16[8,6144]{1,0:T(8,128)(2,1)}, u32[]{:S(2)}) copy-start(bf16[8,6144]{1,0:T(8,128)(2,1)} %param.9) | copy-start | bytes 294916
  51.3 253.4 %all-gather.6.cloned.1.call-start = ((), (), s32[]{:S(2)}) async-start(), calls=%async_computation.2 | async-start | bytes 6389760 | tf_op jit(solution)/shard_map/all_gather | solution.py:71
  52.3 529.3 %reduce-scatter.4.cloned.1.call-start = ((), (), s32[]{:S(2)}) async-start(), calls=%async_computation.3 | async-start | bytes 4259840
  304.7 5.3 copy-start.2
  338.2 2.6 copy-start.3
Sparse Core Ops, SparseCore 0:
  51.5 127.5 all-gather.3
  181.2 123.4 all-gather.5
  351.7 229.8 reduce-scatter.3
where the time goes:
time: 595 us; the launch traced here: 592 us
  waiting for transfers between devices  374 us (63%)
  blocking collectives  170 us (29%)
  between operations  15.7 us (3%)
  matrix products  13.8 us (2%)
  other arithmetic  10.2 us (2%)
  local copies, waits for them, and re-layouts  8 us (1%)
    all_gather x1, waiting for transfers between devices, body(): piece_student = lax.all_gather(student, 'dp', axis=0, tiled=True)  127 us
    all_gather x1, waiting for transfers between devices, body(): piece_target = lax.all_gather(target, 'dp', axis=0, tiled=True)  124 us
    unnamed x4, waiting for transfers between devices  123 us
    psum x1, blocking collectives, body(): loss_value = lax.psum(sum_part, ('dp', 'fsdp')) / image_count  107 us
    psum x1, blocking collectives, body(): embedding = token_mean + lax.psum(partial_value, 'fsdp') + b_out  35.8 us
    all_gather x1, blocking collectives, body(): grad_sum = lax.all_gather(grad_acc, 'fsdp', axis=0, tiled=True)  28 us
  transfers between devices with their start and end apart: 3, of which 3 were waited for; matrix products, arithmetic and copies ran while one was open for 0% of the time, Pallas kernels for 0%

commit v1 on v0

v1 whole, which is shorter than its diff:
```python
import jax
import jax.numpy as jnp
from jax import lax
from jax.experimental import pallas as pl
from jax.experimental.pallas import tpu as pltpu
from jax.sharding import PartitionSpec as P

MESH = pl.DeviceIdType.MESH
F32 = jnp.float32
BF16 = jnp.bfloat16

NZ = 16
NF = 8
NP = 32
LOSS_SCALE = 4096.0
IMAGES = 512
PER_IMAGE = 128
D = 1024
DT = 6144
HID = 512


def dot(left, right):
    return jnp.dot(left, right, preferred_element_type=F32)


def dot_last(left, right):
    return lax.dot_general(left, right, (((1,), (1,)), ((), ())), preferred_element_type=F32)


def dot_first(left, right):
    return lax.dot_general(left, right, (((0,), (0,)), ((), ())), preferred_element_type=F32)


def dot_exact(values, ones):
    high = values.astype(BF16)
    rest = values - high.astype(F32)
    mid = rest.astype(BF16)
    low = (rest - mid.astype(F32)).astype(BF16)
    return dot(high, ones) + dot(mid, ones) + dot(low, ones)


def iota(shape, axis):
    return lax.broadcasted_iota(jnp.int32, shape, axis)


def gelu_parts(values):
    inner = 0.7978845608 * (values + 0.044715 * values * values * values)
    return jnp.tanh(inner)


def kernel(
    tok, tea, ng, win, b_in, wout, b_out, fg,
    loss_ref, gin_ref, gout_ref,
    normed, pre, slope, dhid, tmean, pooled_f, part64, tm64,
    tflat, tp, tj, trow, c1b, st_row, sp, sj, dref, da, dmsg, db,
    px, pin, pout16, pall, zmsg, dz,
    own, sib, coreb, xs, xb, totf, zs, zb,
    s_tq, r_tq, s_tz, r_tz, s_c1, r_c1, s_px, r_px, s_cz, r_cz, s_cp, r_cp,
    s_da, r_da, s_db, r_db, s_pz, r_pz, s_pc, r_pc, s_dz, r_dz,
    s_co, r_co, s_x, r_x, s_z, r_z,
):
    d = lax.axis_index("dp")
    f = lax.axis_index("fsdp")
    xl = d // (2 * NZ)
    z = (d // 2) % NZ
    c = d % 2
    q = xl * 2 + c
    p = q * NF + f

    def dev(xx, zz, cc, ff):
        return ((xx * NZ + zz) * 2 + cc, ff)

    def plane(k):
        qq = (q + k // NF) % 4
        ff = (f + k % NF) % NF
        return qq, ff, qq * NF + ff

    def copy(src, dst, ss, rs, to):
        return pltpu.make_async_remote_copy(
            src_ref=src, dst_ref=dst, send_sem=ss, recv_sem=rs, device_id=to, device_id_type=MESH
        )

    def each(lo, hi, fn):
        def step(k, carry):
            fn(k)
            return carry

        lax.fori_loop(lo, hi, step, 0)

    barrier = pltpu.get_barrier_semaphore()

    def sig_plane(k):
        qq, ff, _ = plane(k)
        pl.semaphore_signal(
            barrier, inc=1, device_id=dev(qq // 2, z, qq % 2, ff), device_id_type=MESH
        )

    def sig_z(k):
        pl.semaphore_signal(
            barrier, inc=1, device_id=dev(xl, (z + k) % NZ, c, f), device_id_type=MESH
        )

    each(1, NP, sig_plane)
    each(1, NZ, sig_z)

    teacher = tea[...].astype(F32)
    t_norm = jnp.sqrt(jnp.sum(teacher * teacher, axis=-1, keepdims=True) + 1e-06)
    target = teacher / t_norm
    for a in range(16):
        for b in range(3):
            lo = 384 * a + 128 * b
            tflat[b, pl.ds(a, 8, stride=16), :] = target[:, lo : lo + 128]
    tp[q] = jnp.concatenate([tflat[b] for b in range(3)], axis=1).astype(BF16)
    own_rows = pl.ds(pl.multiple_of(f * 16, 16), 16)
    own_target = jnp.concatenate([tflat[b, own_rows, :] for b in range(3)], axis=1).astype(BF16)
    trow[...] = own_target
    tj[z] = own_target

    pl.semaphore_wait(barrier, NP - 1 + NZ - 1)

    def tq_copy(k):
        qq = (q + k) % 4
        return copy(
            tp.at[q], tp.at[q], s_tq.at[k], r_tq.at[q], dev(qq // 2, z, qq % 2, f)
        )

    def tz_copy(k):
        return copy(trow, tj.at[z], s_tz.at[k], r_tz.at[z], dev(xl, (z + k) % NZ, c, f))

    each(1, NZ, lambda k: tz_copy(k).start())
    each(1, 4, lambda k: tq_copy(k).start())

    gain = ng[...]
    bias = b_in[...]

    def forward(i):
        rows = pl.ds(pl.multiple_of(i * 256, 256), 256)
        x = tok[rows, :].astype(F32)
        tmean[pl.ds(2 * i, 1), :] = jnp.sum(x[:128], axis=0, keepdims=True) * (1.0 / PER_IMAGE)
        tmean[pl.ds(2 * i + 1, 1), :] = jnp.sum(x[128:], axis=0, keepdims=True) * (1.0 / PER_IMAGE)
        centered = x - jnp.mean(x, axis=-1, keepdims=True)
        inv = lax.rsqrt(jnp.mean(centered * centered, axis=-1, keepdims=True) + 1e-05)
        nb = (centered * inv * gain).astype(BF16)
        normed[rows, :] = nb
        act = dot(nb, win[...]) + bias
        pre[rows, :] = act
        g = 0.5 * act * (1.0 + gelu_parts(act))
        pooled_f[pl.ds(2 * i, 1), :] = jnp.sum(g[:128], axis=0, keepdims=True) * (1.0 / PER_IMAGE)
        pooled_f[pl.ds(2 * i + 1, 1), :] = jnp.sum(g[128:], axis=0, keepdims=True) * (
            1.0 / PER_IMAGE
        )

    each(0, 4, forward)
    pooled_b = pooled_f[...].astype(BF16)
    partial = dot_last(pooled_b, wout[...])
    mean_tok = tmean[...]
    for a in range(8):
        part64[pl.ds(a, 8, stride=8), :] = partial[:, 128 * a : 128 * a + 128]
        tm64[pl.ds(a, 8, stride=8), :] = mean_tok[:, 128 * a : 128 * a + 128]

    def c1_copy(k):
        ff = (f + k) % NF
        return copy(
            part64.at[pl.ds(pl.multiple_of(ff * 8, 8), 8)],
            c1b.at[f], s_c1.at[k], r_c1.at[f], (d, ff),
        )

    each(1, NF, lambda k: c1_copy(k).start())
    c1b[f] = part64[pl.ds(pl.multiple_of(f * 8, 8), 8), :]
    px[...] = pooled_b.astype(F32)

    def px_copy():
        return copy(px, pin, s_px, r_px, dev(1 - xl, z, c, f))

    px_copy().start()

    def slopes(i):
        rows = pl.ds(pl.multiple_of(i * 128, 128), 128)
        v = pre[rows, :]
        t = gelu_parts(v)
        slope[rows, :] = 0.5 * (1.0 + t) + 0.5 * v * (1.0 - t * t) * 0.7978845608 * (
            1.0 + 3.0 * 0.044715 * v * v
        )

    each(0, 8, slopes)

    def wait_from(dst, ss, rs):
        copy(dst, dst, ss, rs, (d, f)).wait_recv()

    def c1_wait(k):
        ff = (f + k) % NF
        wait_from(c1b.at[ff], s_c1.at[k], r_c1.at[ff])

    each(1, NF, c1_wait)
    embedding = jnp.sum(c1b[...], axis=0) + tm64[pl.ds(pl.multiple_of(f * 8, 8), 8), :] + b_out[...]
    final_gain = fg[...]

    def total(v):
        return jnp.sum(jnp.sum(v, axis=1, keepdims=True), axis=0, keepdims=True)

    cent = embedding - total(embedding) * (1.0 / D)
    inv_std = lax.rsqrt(total(cent * cent) * (1.0 / D) + 1e-05)
    n_emb = cent * inv_std
    unit = n_emb * final_gain
    unit_norm = jnp.sqrt(total(unit * unit) + 1e-06)
    unit_dir = unit / unit_norm
    student = unit_dir.astype(BF16).astype(F32)
    st_row[...] = student

    def cz_copy(k):
        return copy(st_row, sj.at[z], s_cz.at[k], r_cz.at[z], dev(xl, (z + k) % NZ, c, f))

    def cp_copy(k):
        qq, ff, _ = plane(k)
        return copy(st_row, sp.at[p], s_cp.at[k], r_cp.at[p], dev(qq // 2, z, qq % 2, ff))

    each(1, NZ, lambda k: cz_copy(k).start())
    each(1, NP, lambda k: cp_copy(k).start())
    sj[z] = student
    sp[p] = student

    def tq_wait(k):
        qq = (q + k) % 4
        wait_from(tp.at[qq], s_tq.at[k], r_tq.at[qq])

    def tz_wait(k):
        zz = (z + k) % NZ
        wait_from(tj.at[zz], s_tz.at[k], r_tz.at[zz])

    each(1, 4, tq_wait)
    each(1, NZ, tz_wait)
    tx = dot_last(tp[...].reshape(NP * 16, 384), tj[...].reshape(NZ * 16, 384))
    same = (iota(tx.shape, 0) % 16) == (iota(tx.shape, 1) % 16)
    tx = jnp.sum(jnp.where(same, tx, 0.0).reshape(NP, 16, NZ * 16), axis=1)
    spread = ((iota((NZ * 16, 128), 0) // 16) == (iota((NZ * 16, 128), 1) // 8)).astype(BF16)
    gram_t = dot_exact(tx, spread)

    def pz_copy(k):
        return copy(
            pout16, pall.at[c, z], s_pz.at[k], r_pz.at[z], dev(xl, (z + k) % NZ, c, f)
        )

    wait_from(pin, s_px, r_px)
    mine, other = px[...], pin[...]
    first = xl == 0
    block16 = jnp.concatenate(
        [jnp.where(first, mine, other), jnp.where(first, other, mine)], axis=0
    ).astype(BF16)
    pout16[...] = block16
    pall[c, z] = block16

    def cz_wait(k):
        zz = (z + k) % NZ
        wait_from(sj.at[zz], s_cz.at[k], r_cz.at[zz])

    def cp_wait(k):
        _, _, pp = plane(k)
        wait_from(sp.at[pp], s_cp.at[k], r_cp.at[pp])

    each(1, NP, cp_wait)
    each(1, NZ, cz_wait)
    s_plane = sp[...].reshape(NP * 8, 128).astype(BF16)
    s_other = sj[...].reshape(NZ * 8, 128).astype(BF16)
    sx = dot_last(s_plane, s_other)
    diag = (iota(sx.shape, 0) % 8) == (iota(sx.shape, 1) % 8)
    sx = jnp.sum(jnp.where(diag, sx, 0.0).reshape(NP, 8, 128), axis=1)
    group = ((iota((128, 128), 0) // 8) == (iota((128, 128), 1) // 8)).astype(BF16)
    resid = dot_exact(sx, group) - gram_t
    share = total(resid * resid) * 0.125
    wide = jnp.broadcast_to(resid[:, None, :], (NP, 8, 128)).reshape(NP * 8, 128)
    wide = jnp.where(diag, wide, 0.0).astype(BF16)
    dref[...] = dot(wide, s_other).reshape(NP, 8, 128)

    def da_copy(k):
        qq, ff, pp = plane(k)
        return copy(dref.at[pp], da.at[p], s_da.at[k], r_da.at[p], dev(qq // 2, z, qq % 2, ff))

    each(1, NP, lambda k: da_copy(k).start())
    da[p] = dref[p]
    each(1, NZ, lambda k: pz_copy(k).start())

    def da_wait(k):
        _, _, pp = plane(k)
        wait_from(da.at[pp], s_da.at[k], r_da.at[pp])

    each(1, NP, da_wait)
    dstudent = (LOSS_SCALE * 4.0 / IMAGES) * jnp.sum(da[...], axis=0)
    dunit = (dstudent - unit_dir * total(unit_dir * dstudent)) / unit_norm
    gain_grad = dunit * final_gain
    dembed = inv_std * (
        gain_grad - total(gain_grad) * (1.0 / D) - n_emb * (total(gain_grad * n_emb) * (1.0 / D))
    )
    message = jnp.concatenate(
        [dembed.astype(BF16).astype(F32), jnp.broadcast_to(share, (8, 128))], axis=0
    )
    dmsg[...] = message

    def rows16(pp):
        return pl.ds(pl.multiple_of(pp * 16, 16), 16)

    def db_copy(k):
        qq, ff, _ = plane(k)
        return copy(
            dmsg, db.at[rows16(p)], s_db.at[k], r_db.at[p], dev(qq // 2, z, qq % 2, ff)
        )

    each(1, NP, lambda k: db_copy(k).start())
    db[rows16(p), :] = message

    def db_wait(k):
        _, _, pp = plane(k)
        wait_from(db.at[rows16(pp)], s_db.at[k], r_db.at[pp])

    each(1, NF, db_wait)
    block = jnp.concatenate(
        [db[pl.ds(q * (NF * 16) + a, 8, stride=16), :] for a in range(8)], axis=1
    ).astype(BF16)
    tmean[:, :HID] = dot(block, wout[...]) * (1.0 / PER_IMAGE)

    def hidden(i):
        rows = pl.ds(pl.multiple_of(i * PER_IMAGE, PER_IMAGE), PER_IMAGE)
        dhid[rows, :] = (tmean[pl.ds(i, 1), :HID] * slope[rows, :]).astype(BF16)

    each(0, 8, hidden)

    low = c == 0

    def co_copy(j):
        return copy(sib.at[j], coreb.at[j], s_co.at[j], r_co.at[j], dev(xl, z, 1 - c, f))

    def x_copy(j):
        return copy(xs.at[j], xb.at[j], s_x.at[j], r_x.at[j], dev(1 - xl, z, c, f))

    for j in range(4):
        side = (1 - xl) if j < 2 else xl
        cols = pl.ds(pl.multiple_of(side * 512 + (j % 2) * 256, 256), 256)
        term = dot_first(normed[:, cols], dhid[...]).reshape(8, 2, 16, HID)
        own[j] = jnp.where(low, term[:, 0], term[:, 1])
        sib[j] = jnp.where(low, term[:, 1], term[:, 0]).astype(BF16)
        co_copy(j).start()
        if j >= 1 and j <= 2:
            wait_from(coreb.at[j - 1], s_co.at[j - 1], r_co.at[j - 1])
            xs[j - 1] = (own[j - 1] + coreb[j - 1].astype(F32)).astype(BF16)
            x_copy(j - 1).start()

    each(NF, NP, db_wait)
    loss_plane = jnp.zeros((8, 128), F32)
    for pp in range(NP):
        loss_plane = loss_plane + db[pp * 16 + 8 : pp * 16 + 16, :]
    flat = jnp.concatenate(
        [db[pl.ds(xl * 4 + a, NP, stride=16), :] for a in range(4)], axis=1
    ).astype(BF16)
    image = iota((NP, 128), 0)
    lane = ((image // 8) % 2) * 64 + (z % 4) * 16 + (image // 16) * 8 + image % 8
    place = (lane == iota((NP, 128), 1)).astype(BF16)
    turned = dot_first(flat, place).reshape(NZ, 2, 16, 128)
    zmsg[:, 0:16, :] = jnp.where(low, turned[:, 0], turned[:, 1])
    zmsg[:, 16:24, :] = jnp.broadcast_to(loss_plane[None], (NZ, 8, 128))
    dz[z] = zmsg[z]

    def dz_copy(k):
        zz = (z + k) % NZ
        return copy(zmsg.at[zz], dz.at[z], s_dz.at[k], r_dz.at[z], dev(xl, zz, c, f))

    each(1, NZ, lambda k: dz_copy(k).start())

    def z_copy(zz):
        return copy(zs.at[zz], zb.at[z], s_z.at[zz], r_z.at[z], dev(xl, zz, c, f))

    zb[z] = jnp.zeros((16, HID), BF16)
    for h in range(2):
        j = 2 + h
        wait_from(coreb.at[j], s_co.at[j], r_co.at[j])
        wait_from(xb.at[h], s_x.at[h], r_x.at[h])
        merged = own[j] + coreb[j].astype(F32) + xb[h].astype(F32)
        totf[8 * h : 8 * h + 8] = merged
        zs[8 * h : 8 * h + 8] = merged.astype(BF16)

        def z_start(zz):
            @pl.when(zz != z)
            def _():
                z_copy(zz).start()

        each(8 * h, 8 * h + 8, z_start)

    def pz_wait(k):
        zz = (z + k) % NZ
        wait_from(pall.at[c, zz], s_pz.at[k], r_pz.at[zz])

    each(1, NZ, pz_wait)

    def pc_copy():
        return copy(pall.at[c], pall.at[c], s_pc, r_pc, dev(xl, z, 1 - c, f))

    pc_copy().start()

    def dz_wait(k):
        zz = (z + k) % NZ
        wait_from(dz.at[zz], s_dz.at[k], r_dz.at[zz])

    each(1, NZ, dz_wait)
    wait_from(pall.at[1 - c], s_pc, r_pc)
    acc = jnp.zeros((16, HID), F32)
    loss = jnp.zeros((8, 128), F32)
    for g in range(NZ // 4):
        left = jnp.zeros((16, 128), F32)
        for zz in range(4 * g, 4 * g + 4):
            left = left + dz[zz, 0:16, :]
            loss = loss + dz[zz, 16:24, :]
        right = jnp.concatenate(
            [pall[cc, 4 * g : 4 * g + 4].reshape(64, HID) for cc in range(2)], axis=0
        )
        acc = acc + dot(left.astype(BF16), right)
    gout_ref[...] = acc.astype(BF16)
    loss_ref[...] = loss * (1.0 / IMAGES)

    def z_wait(k):
        zz = (z + k) % NZ
        wait_from(zb.at[zz], s_z.at[zz], r_z.at[zz])

    each(1, NZ, z_wait)
    gin_ref[...] = (totf[z] + jnp.sum(zb[...].astype(F32), axis=0)).astype(BF16)

    each(1, 4, lambda k: tq_copy(k).wait_send())
    each(1, NZ, lambda k: tz_copy(k).wait_send())
    each(1, NF, lambda k: c1_copy(k).wait_send())
    px_copy().wait_send()
    each(1, NZ, lambda k: cz_copy(k).wait_send())
    each(1, NP, lambda k: cp_copy(k).wait_send())
    each(1, NP, lambda k: da_copy(k).wait_send())
    each(1, NZ, lambda k: pz_copy(k).wait_send())
    each(1, NP, lambda k: db_copy(k).wait_send())
    each(1, NZ, lambda k: dz_copy(k).wait_send())
    each(0, 4, lambda j: co_copy(j).wait_send())
    each(0, 2, lambda j: x_copy(j).wait_send())
    each(1, NZ, lambda k: z_copy((z + k) % NZ).wait_send())
    pc_copy().wait_send()


def body(tokens, teacher, norm_gain, w_in, b_in, w_out, b_out, final_gain):
    vmem = pl.BlockSpec(memory_space=pltpu.VMEM)
    sems = []
    for n in (4, NZ, NF, None, NZ, NP, NP, NP, NZ, None, NZ, 4, 2, NZ):
        sems += [pltpu.SemaphoreType.DMA if n is None else pltpu.SemaphoreType.DMA((n,))] * 2
    loss, grad_in, grad_out = pl.pallas_call(
        kernel,
        name="gram_step",
        out_shape=(
            jax.ShapeDtypeStruct((8, 128), F32),
            jax.ShapeDtypeStruct((16, HID), BF16),
            jax.ShapeDtypeStruct((16, HID), BF16),
        ),
        in_specs=[vmem] * 8,
        out_specs=(vmem, vmem, vmem),
        scratch_shapes=[
            pltpu.VMEM((1024, D), BF16),
            pltpu.VMEM((1024, HID), F32),
            pltpu.VMEM((1024, HID), F32),
            pltpu.VMEM((1024, HID), BF16),
            pltpu.VMEM((8, D), F32),
            pltpu.VMEM((8, HID), F32),
            pltpu.VMEM((64, 128), F32),
            pltpu.VMEM((64, 128), F32),
            pltpu.VMEM((3, 128, 128), F32),
            pltpu.VMEM((4, 128, 384), BF16),
            pltpu.VMEM((NZ, 16, 384), BF16),
            pltpu.VMEM((16, 384), BF16),
            pltpu.VMEM((NF, 8, 128), F32),
            pltpu.VMEM((8, 128), F32),
            pltpu.VMEM((NP, 8, 128), F32),
            pltpu.VMEM((NZ, 8, 128), F32),
            pltpu.VMEM((NP, 8, 128), F32),
            pltpu.VMEM((NP, 8, 128), F32),
            pltpu.VMEM((16, 128), F32),
            pltpu.VMEM((NP * 16, 128), F32),
            pltpu.VMEM((8, HID), F32),
            pltpu.VMEM((8, HID), F32),
            pltpu.VMEM((16, HID), BF16),
            pltpu.VMEM((2, NZ, 16, HID), BF16),
            pltpu.VMEM((NZ, 24, 128), F32),
            pltpu.VMEM((NZ, 24, 128), F32),
            pltpu.VMEM((4, 8, 16, HID), F32),
            pltpu.VMEM((4, 8, 16, HID), BF16),
            pltpu.VMEM((4, 8, 16, HID), BF16),
            pltpu.VMEM((2, 8, 16, HID), BF16),
            pltpu.VMEM((2, 8, 16, HID), BF16),
            pltpu.VMEM((NZ, 16, HID), F32),
            pltpu.VMEM((NZ, 16, HID), BF16),
            pltpu.VMEM((NZ, 16, HID), BF16),
        ]
        + sems,
        compiler_params=pltpu.CompilerParams(
            collective_id=0, has_side_effects=True, vmem_limit_bytes=48 << 20
        ),
        cost_estimate=pl.CostEstimate(
            flops=5_000_000_000, bytes_accessed=8_000_000, transcendentals=1_000_000
        ),
    )(
        tokens,
        teacher,
        norm_gain.reshape(1, D),
        w_in,
        b_in.reshape(1, HID),
        w_out,
        b_out.reshape(8, 128),
        final_gain.reshape(8, 128),
    )
    return loss[0, 0], grad_in, grad_out


def solution(mesh):
    return jax.shard_map(
        body,
        mesh=mesh,
        in_specs=(
            P("dp", None),
            P("dp", None),
            P(),
            P(None, "fsdp"),
            P("fsdp"),
            P(None, "fsdp"),
            P(),
            P(),
        ),
        out_specs=(P(), P("dp", "fsdp"), P("dp", "fsdp")),
        check_vma=False,
    )
```

time: 595 us -> 84.6 us (0.14)
  the two profiles are of different devices: /device:TPU:1 before, /device:TPU:33 now
where the time goes in v1:
time: 84.6 us; the launch traced here: 84.2 us
  Pallas kernels  74.2 us (88%)
  local copies, waits for them, and re-layouts  9.39 us (11%)
    pallas_call x1, Pallas kernels, body(): pl.pallas_call(kernel, name='gram_step', out_shape=(jax.ShapeDtypeStruct(...  74.2 us
    unnamed x18, local copies, waits for them, and re-layouts  8.87 us

profile of v1, /device:TPU:33, one launch (start us, length us, event | category | flops | bytes accessed | tf_op | source)
XLA Modules:
  0.0 84.2 jit_solution(14985299597734342554)
XLA Ops:
  0.6 0.0 copy-start
  0.6 1.6 %copy-done = bf16[1024,1024]{1,0:T(8,128)(2,1)S(1)} copy-done((bf16[1024,1024]{1,0:T(8,128)(2,1)S(1)}, bf16[1024,1024]{1,0:T(8,128)(2,1)}, u32[]{:S(2)}) %copy-start) | copy-done | bytes 2097176
  2.2 0.0 copy-start.1
  2.2 1.2 %copy-done.1 = bf16[1024,512]{1,0:T(8,128)(2,1)S(1)} copy-done((bf16[1024,512]{1,0:T(8,128)(2,1)S(1)}, bf16[1024,512]{1,0:T(8,128)(2,1)}, u32[]{:S(2)}) %copy-start.1) | copy-done | bytes 1048600
  3.5 0.0 copy-start.2
  3.5 1.2 %copy-done.2 = bf16[1024,512]{1,0:T(8,128)(2,1)S(1)} copy-done((bf16[1024,512]{1,0:T(8,128)(2,1)S(1)}, bf16[1024,512]{1,0:T(8,128)(2,1)}, u32[]{:S(2)}) %copy-start.2) | copy-done | bytes 1048600
  4.7 0.0 copy-start.3
  4.7 0.9 %copy-done.3 = bf16[8,6144]{1,0:T(8,128)(2,1)S(1)} copy-done((bf16[8,6144]{1,0:T(8,128)(2,1)S(1)}, bf16[8,6144]{1,0:T(8,128)(2,1)}, u32[]{:S(2)}) %copy-start.3) | copy-done | bytes 98328
  5.6 0.0 copy-start.4
  5.6 0.7 copy-done.4
  6.3 0.0 copy-start.5
  6.3 0.7 copy-done.5
  6.9 0.0 copy-start.6
  6.9 0.7 copy-done.6
  7.6 0.0 copy-start.7
  7.6 0.7 copy-done.7
  8.3 74.2 %gram_step.1 = (f32[8,128]{1,0:T(8,128)S(1)}, bf16[16,512]{1,0:T(8,128)(2,1)S(1)}, bf16[16,512]{1,0:T(8,128)(2,1)S(1)}) custom-call(bf16[1024,1024]{1,0:T(8,128)(2,1)S(1)} %copy-done, bf16[8,6144]{1,0:T(8,128)(2,1)S(1)} %copy-done.3, f32[1,1024]{1,0:T(1,128)S(1)} %bitcast.5, bf16[1024,512]{1,0:T(8,128)(2,1)S(1)} %copy-done.1, f32[1,512]{1,0:T(1,128)S(1)} %bitcast.8, ...), custom_call_target="tpu_custom_call" | custom-call | flops 5000000000 | bytes 8000000 | tf_op jit(solution)/shard_map/gram_step/pallas_call | solution.py:446
  82.5 0.5 slice.3
  83.0 0.6 copy.13
  83.6 0.6 copy.14
Async XLA Ops:
  0.6 1.6 %copy-start = (bf16[1024,1024]{1,0:T(8,128)(2,1)S(1)}, bf16[1024,1024]{1,0:T(8,128)(2,1)}, u32[]{:S(2)}) copy-start(bf16[1024,1024]{1,0:T(8,128)(2,1)} %tok.1) | copy-start | bytes 6291460
  2.2 1.2 %copy-start.1 = (bf16[1024,512]{1,0:T(8,128)(2,1)S(1)}, bf16[1024,512]{1,0:T(8,128)(2,1)}, u32[]{:S(2)}) copy-start(bf16[1024,512]{1,0:T(8,128)(2,1)} %win.1) | copy-start | bytes 3145732
  3.5 1.2 %copy-start.2 = (bf16[1024,512]{1,0:T(8,128)(2,1)S(1)}, bf16[1024,512]{1,0:T(8,128)(2,1)}, u32[]{:S(2)}) copy-start(bf16[1024,512]{1,0:T(8,128)(2,1)} %wout.1) | copy-start | bytes 3145732
  4.7 0.9 %copy-start.3 = (bf16[8,6144]{1,0:T(8,128)(2,1)S(1)}, bf16[8,6144]{1,0:T(8,128)(2,1)}, u32[]{:S(2)}) copy-start(bf16[8,6144]{1,0:T(8,128)(2,1)} %tea.1) | copy-start | bytes 294916
  5.6 0.7 copy-start.4
  6.3 0.7 copy-start.5
  6.9 0.7 copy-start.6
  7.6 0.7 copy-start.7

commit v2 on v1

v2 whole, which is shorter than its diff:
```python
import jax
import jax.numpy as jnp
from jax import lax
from jax.experimental import pallas as pl
from jax.experimental.pallas import tpu as pltpu
from jax.sharding import PartitionSpec as P

MESH = pl.DeviceIdType.MESH
F32 = jnp.float32
BF16 = jnp.bfloat16

NZ = 16
NF = 8
NW = 8
NP = 32
LOSS_SCALE = 4096.0
IMAGES = 512
PER_IMAGE = 128
D = 1024
DT = 6144
HID = 512


def dot(left, right):
    return jnp.dot(left, right, preferred_element_type=F32)


def dot_last(left, right):
    return lax.dot_general(left, right, (((1,), (1,)), ((), ())), preferred_element_type=F32)


def dot_first(left, right):
    return lax.dot_general(left, right, (((0,), (0,)), ((), ())), preferred_element_type=F32)


def dot_exact(values, ones):
    high = values.astype(BF16)
    rest = values - high.astype(F32)
    mid = rest.astype(BF16)
    low = (rest - mid.astype(F32)).astype(BF16)
    return dot(high, ones) + dot(mid, ones) + dot(low, ones)


def div(value, by):
    return lax.div(value, jnp.int32(by))


def rem(value, by):
    return lax.rem(value, jnp.int32(by))


def iota(shape, axis):
    return lax.broadcasted_iota(jnp.int32, shape, axis)


def gelu_parts(values):
    inner = 0.7978845608 * (values + 0.044715 * values * values * values)
    return jnp.tanh(inner)


def kernel(
    tok_h, tea_h, ng_h, win_h, b_in_h, wout_h, b_out_h, fg_h,
    out_ref, loss_ref,
    tok, tea, ng, win, b_in, wout, b_out, fg, s_in,
    normed, pre, slope, dhid, tmean, pooled_f, part64, tm64,
    tflat, tp, tj, trow, c1b, st_row, sp, sj, dref, da, dmsg, db,
    px, pin, pout16, pall, zmsg, dz,
    own, sib, coreb, xs, xb, totf, zs, zb,
    s_tq, r_tq, s_tz, r_tz, s_c1, r_c1, s_px, r_px, s_cz, r_cz, s_cp, r_cp,
    s_da, r_da, s_db, r_db, s_pz, r_pz, s_pc, r_pc, s_dz, r_dz,
    s_co, r_co, s_x, r_x, s_z, r_z,
):
    d = lax.axis_index("dp")
    f = lax.axis_index("fsdp")
    xl = div(d, 2 * NZ)
    z = rem(div(d, 2), NZ)
    c = rem(d, 2)
    q = xl * 2 + c
    p = q * NF + f

    def dev(xx, zz, cc, ff):
        return ((xx * NZ + zz) * 2 + cc, ff)

    def plane(k):
        qq = rem(q + div(k, NF), 4)
        ff = rem(f + rem(k, NF), NF)
        return qq, ff, qq * NF + ff

    def copy(src, dst, ss, rs, to):
        return pltpu.make_async_remote_copy(
            src_ref=src, dst_ref=dst, send_sem=ss, recv_sem=rs, device_id=to, device_id_type=MESH
        )

    def each(lo, hi, fn):
        def step(k, carry):
            fn(k)
            return carry

        lax.fori_loop(lo, hi, step, 0)

    def load(n, src, dst):
        return pltpu.make_async_copy(src, dst, s_in.at[n])

    def load_tok(i):
        rows = pl.ds(pl.multiple_of(i * 256, 256), 256)
        return load(i, tok_h.at[rows], tok.at[rows])

    loads = [
        load(4 + n, src, dst)
        for n, (src, dst) in enumerate(
            [
                (tea_h, tea), (ng_h, ng), (win_h, win), (b_in_h, b_in),
                (wout_h, wout), (b_out_h, b_out), (fg_h, fg),
            ]
        )
    ]
    loads[0].start()
    loads[1].start()
    load_tok(0).start()
    loads[2].start()
    loads[3].start()
    each(1, 4, lambda i: load_tok(i).start())
    for item in loads[4:]:
        item.start()

    barrier = pltpu.get_barrier_semaphore()

    def sig_plane(k):
        qq, ff, _ = plane(k)
        pl.semaphore_signal(
            barrier, inc=1, device_id=dev(div(qq, 2), z, rem(qq, 2), ff), device_id_type=MESH
        )

    def sig_z(k):
        pl.semaphore_signal(
            barrier, inc=1, device_id=dev(xl, rem(z + k, NZ), c, f), device_id_type=MESH
        )

    each(1, NP, sig_plane)
    each(1, NZ, sig_z)

    loads[0].wait()
    teacher = tea[...].astype(F32)
    t_norm = jnp.sqrt(jnp.sum(teacher * teacher, axis=-1, keepdims=True) + 1e-06)
    target = teacher / t_norm
    for a in range(16):
        for b in range(3):
            lo = 384 * a + 128 * b
            tflat[b, pl.ds(a, 8, stride=16), :] = target[:, lo : lo + 128]
    tp[q] = jnp.concatenate([tflat[b] for b in range(3)], axis=1).astype(BF16)
    own_rows = pl.ds(pl.multiple_of(f * 16, 16), 16)
    own_target = jnp.concatenate([tflat[b, own_rows, :] for b in range(3)], axis=1).astype(BF16)
    trow[...] = own_target
    tj[z] = own_target

    for item in loads[1:4]:
        item.wait()
    gain = ng[...]
    bias = b_in[...]

    def forward(i):
        load_tok(i).wait()
        rows = pl.ds(pl.multiple_of(i * 256, 256), 256)
        x = tok[rows, :].astype(F32)
        tmean[pl.ds(2 * i, 1), :] = jnp.sum(x[:128], axis=0, keepdims=True) * (1.0 / PER_IMAGE)
        tmean[pl.ds(2 * i + 1, 1), :] = jnp.sum(x[128:], axis=0, keepdims=True) * (1.0 / PER_IMAGE)
        centered = x - jnp.mean(x, axis=-1, keepdims=True)
        inv = lax.rsqrt(jnp.mean(centered * centered, axis=-1, keepdims=True) + 1e-05)
        nb = (centered * inv * gain).astype(BF16)
        normed[rows, :] = nb
        act = dot(nb, win[...]) + bias
        pre[rows, :] = act
        g = 0.5 * act * (1.0 + gelu_parts(act))
        pooled_f[pl.ds(2 * i, 1), :] = jnp.sum(g[:128], axis=0, keepdims=True) * (1.0 / PER_IMAGE)
        pooled_f[pl.ds(2 * i + 1, 1), :] = jnp.sum(g[128:], axis=0, keepdims=True) * (
            1.0 / PER_IMAGE
        )

    each(0, 2, forward)
    pl.semaphore_wait(barrier, NP - 1 + NZ - 1)
    def tq_copy(k):
        qq = rem(q + k, 4)
        return copy(
            tp.at[q], tp.at[q], s_tq, r_tq, dev(div(qq, 2), z, rem(qq, 2), f)
        )

    def tz_copy(k):
        return copy(trow, tj.at[z], s_tz, r_tz, dev(xl, rem(z + k, NZ), c, f))

    each(1, NZ, lambda k: tz_copy(k).start())
    each(1, 4, lambda k: tq_copy(k).start())
    each(2, 4, forward)
    for item in loads[4:]:
        item.wait()
    pooled_b = pooled_f[...].astype(BF16)
    partial = dot_last(pooled_b, wout[...])
    mean_tok = tmean[...]
    for a in range(8):
        part64[pl.ds(a, 8, stride=8), :] = partial[:, 128 * a : 128 * a + 128]
        tm64[pl.ds(a, 8, stride=8), :] = mean_tok[:, 128 * a : 128 * a + 128]

    def c1_copy(k):
        ff = rem(f + k, NF)
        return copy(
            part64.at[pl.ds(pl.multiple_of(ff * 8, 8), 8)],
            c1b.at[f], s_c1, r_c1, (d, ff),
        )

    each(1, NF, lambda k: c1_copy(k).start())
    c1b[f] = part64[pl.ds(pl.multiple_of(f * 8, 8), 8), :]
    px[...] = pooled_b.astype(F32)

    def px_copy():
        return copy(px, pin, s_px, r_px, dev(1 - xl, z, c, f))

    px_copy().start()

    def slopes(i):
        rows = pl.ds(pl.multiple_of(i * 128, 128), 128)
        v = pre[rows, :]
        t = gelu_parts(v)
        slope[rows, :] = 0.5 * (1.0 + t) + 0.5 * v * (1.0 - t * t) * 0.7978845608 * (
            1.0 + 3.0 * 0.044715 * v * v
        )

    each(0, 8, slopes)

    def wait_from(dst, ss, rs):
        copy(dst, dst, ss, rs, (d, f)).wait_recv()

    def sent(src, ss, rs):
        copy(src, src, ss, rs, (d, f)).wait_send()

    wait_from(c1b.at[0 : NF - 1], s_c1, r_c1)
    embedding = jnp.sum(c1b[...], axis=0) + tm64[pl.ds(pl.multiple_of(f * 8, 8), 8), :] + b_out[...]
    final_gain = fg[...]

    def total(v):
        return jnp.sum(jnp.sum(v, axis=1, keepdims=True), axis=0, keepdims=True)

    cent = embedding - total(embedding) * (1.0 / D)
    inv_std = lax.rsqrt(total(cent * cent) * (1.0 / D) + 1e-05)
    n_emb = cent * inv_std
    unit = n_emb * final_gain
    unit_norm = jnp.sqrt(total(unit * unit) + 1e-06)
    unit_dir = unit / unit_norm
    student = unit_dir.astype(BF16).astype(F32)
    st_row[...] = student

    def cz_copy(k):
        return copy(st_row, sj.at[z], s_cz, r_cz, dev(xl, rem(z + k, NZ), c, f))

    def cp_copy(k):
        qq, ff, _ = plane(k)
        return copy(st_row, sp.at[p], s_cp, r_cp, dev(div(qq, 2), z, rem(qq, 2), ff))

    each(1, NZ, lambda k: cz_copy(k).start())
    each(1, NP, lambda k: cp_copy(k).start())
    sj[z] = student
    sp[p] = student

    wait_from(tp.at[0:3], s_tq, r_tq)
    wait_from(tj.at[0 : NZ - 1], s_tz, r_tz)
    tx = dot_last(tp[...].reshape(NP * 16, 384), tj[...].reshape(NZ * 16, 384))
    same = (iota(tx.shape, 0) % 16) == (iota(tx.shape, 1) % 16)
    tx = jnp.sum(jnp.where(same, tx, 0.0).reshape(NP, 16, NZ * 16), axis=1)
    spread = ((iota((NZ * 16, 128), 0) // 16) == (iota((NZ * 16, 128), 1) // 8)).astype(BF16)
    gram_t = dot_exact(tx, spread)

    def pz_copy(k):
        return copy(
            pout16, pall.at[c, z], s_pz, r_pz, dev(xl, rem(z + k, NZ), c, f)
        )

    wait_from(pin, s_px, r_px)
    mine, other = px[...], pin[...]
    first = xl == 0
    block16 = jnp.concatenate(
        [jnp.where(first, mine, other), jnp.where(first, other, mine)], axis=0
    ).astype(BF16)
    pout16[...] = block16
    pall[c, z] = block16

    wait_from(sp.at[0 : NP - 1], s_cp, r_cp)
    wait_from(sj.at[0 : NZ - 1], s_cz, r_cz)
    s_plane = sp[...].reshape(NP * 8, 128).astype(BF16)
    s_other = sj[...].reshape(NZ * 8, 128).astype(BF16)
    sx = dot_last(s_plane, s_other)
    diag = (iota(sx.shape, 0) % 8) == (iota(sx.shape, 1) % 8)
    sx = jnp.sum(jnp.where(diag, sx, 0.0).reshape(NP, 8, 128), axis=1)
    group = ((iota((128, 128), 0) // 8) == (iota((128, 128), 1) // 8)).astype(BF16)
    resid = dot_exact(sx, group) - gram_t
    share = total(resid * resid) * 0.125
    wide = jnp.broadcast_to(resid[:, None, :], (NP, 8, 128)).reshape(NP * 8, 128)
    wide = jnp.where(diag, wide, 0.0).astype(BF16)
    dref[...] = dot(wide, s_other).reshape(NP, 8, 128)

    def da_copy(k):
        qq, ff, pp = plane(k)
        return copy(dref.at[pp], da.at[p], s_da, r_da, dev(div(qq, 2), z, rem(qq, 2), ff))

    each(1, NP, lambda k: da_copy(k).start())
    da[p] = dref[p]
    each(1, NZ, lambda k: pz_copy(k).start())

    wait_from(da.at[0 : NP - 1], s_da, r_da)
    dstudent = (LOSS_SCALE * 4.0 / IMAGES) * jnp.sum(da[...], axis=0)
    dunit = (dstudent - unit_dir * total(unit_dir * dstudent)) / unit_norm
    gain_grad = dunit * final_gain
    dembed = inv_std * (
        gain_grad - total(gain_grad) * (1.0 / D) - n_emb * (total(gain_grad * n_emb) * (1.0 / D))
    )
    message = jnp.concatenate(
        [dembed.astype(BF16).astype(F32), jnp.broadcast_to(share, (8, 128))], axis=0
    )
    dmsg[...] = message

    def rows16(pp):
        return pl.ds(pl.multiple_of(pp * 16, 16), 16)

    def db_copy(k, near):
        qq, ff, _ = plane(k)
        return copy(
            dmsg, db.at[rows16(p)], s_db.at[near], r_db.at[near], dev(div(qq, 2), z, rem(qq, 2), ff)
        )

    each(1, NF, lambda k: db_copy(k, 0).start())
    each(NF, NP, lambda k: db_copy(k, 1).start())
    db[rows16(p), :] = message

    wait_from(db.at[0 : (NF - 1) * 16], s_db.at[0], r_db.at[0])
    block = jnp.concatenate(
        [db[pl.ds(q * (NF * 16) + a, 8, stride=16), :] for a in range(8)], axis=1
    ).astype(BF16)
    tmean[:, :HID] = dot(block, wout[...]) * (1.0 / PER_IMAGE)

    def hidden(i):
        rows = pl.ds(pl.multiple_of(i * PER_IMAGE, PER_IMAGE), PER_IMAGE)
        dhid[rows, :] = (tmean[pl.ds(i, 1), :HID] * slope[rows, :]).astype(BF16)

    each(0, 8, hidden)

    low = c == 0
    s_bit = rem(z, 2)
    w = div(z, 2)

    def co_copy(j):
        return copy(sib.at[j], coreb.at[j], s_co, r_co.at[j], dev(xl, z, 1 - c, f))

    def near_copy(t, h):
        xx = xl if t == 2 else 1 - xl
        zz = 2 * w + (s_bit if t == 1 else 1 - s_bit)
        return copy(
            xs.at[t, h], xb.at[h, t], s_x, r_x.at[h], dev(xx, zz, c, f)
        )

    def core_sum(j, bit):
        return own[j, bit] + coreb[j, bit].astype(F32)

    def near_send(j):
        wait_from(coreb.at[j], s_co, r_co.at[j])
        h = j % 2
        for t in (0, 1) if j < 2 else (2,):
            xs[t, h] = core_sum(j, s_bit if t == 1 else 1 - s_bit).astype(BF16)
            near_copy(t, h).start()

    for j in range(4):
        side = (1 - xl) if j < 2 else xl
        cols = pl.ds(pl.multiple_of(side * 512 + (j % 2) * 256, 256), 256)
        term = dot_first(normed[:, cols], dhid[...]).reshape(4, 2, 2, 16, HID)
        for bit in range(2):
            mine_t, other_t = term[:, bit, 0], term[:, bit, 1]
            own[j, bit] = jnp.where(low, mine_t, other_t)
            sib[j, bit] = jnp.where(low, other_t, mine_t).astype(BF16)
        co_copy(j).start()
        if j >= 1:
            near_send(j - 1)

    wait_from(db.at[0 : (NP - NF) * 16], s_db.at[1], r_db.at[1])
    loss_plane = jnp.zeros((8, 128), F32)
    for pp in range(NP):
        loss_plane = loss_plane + db[pp * 16 + 8 : pp * 16 + 16, :]
    flat = jnp.concatenate(
        [db[pl.ds(xl * 4 + a, NP, stride=16), :] for a in range(4)], axis=1
    ).astype(BF16)
    image = iota((NP, 128), 0)
    odd = rem(z, 2)
    lane = odd * 32 + ((image // 8) % 2) * 16 + (image // 16) * 8 + image % 8
    place = (lane == iota((NP, 128), 1)).astype(BF16)
    turned = dot_first(flat, place).reshape(NZ, 2, 16, 128)
    turned = jnp.where(low, turned[:, 0], turned[:, 1])
    part = loss_plane[0:1, :]
    high = part.astype(BF16).astype(F32)
    mid = (part - high).astype(BF16).astype(F32)
    last = part - high - mid
    at = iota((1, 128), 1) - (64 + 4 * odd)
    extra = jnp.where(at == 0, high, jnp.where(at == 1, mid, jnp.where(at == 2, last, 0.0)))
    zmsg[...] = (turned + extra[None]).astype(BF16)
    dz[z] = zmsg[z]

    def dz_copy(k):
        zz = rem(z + k, NZ)
        return copy(zmsg.at[zz], dz.at[z], s_dz, r_dz, dev(xl, zz, c, f))

    each(1, NZ, lambda k: dz_copy(k).start())

    near_send(3)

    def z_copy(k):
        ww = rem(w + k, NW)
        return copy(zs.at[ww], zb.at[w], s_z, r_z, dev(xl, 2 * ww + s_bit, c, f))

    def z_start(k):
        z_copy(k).start()

    zb[w] = jnp.zeros((16, HID), BF16)
    for h in range(2):
        merged = core_sum(2 + h, s_bit)
        wait_from(xb.at[h], s_x, r_x.at[h])
        for t in range(3):
            merged = merged + xb[h, t].astype(F32)
        totf[4 * h : 4 * h + 4] = merged
        zs[4 * h : 4 * h + 4] = merged.astype(BF16)
        for ww in range(4 * h, 4 * h + 4):
            k = rem(ww + NW - w, NW)

            @pl.when(k != 0)
            def _():
                z_start(k)

    wait_from(pall.at[c, 0 : NZ - 1], s_pz, r_pz)

    def pc_copy():
        return copy(pall.at[c], pall.at[c], s_pc, r_pc, dev(xl, z, 1 - c, f))

    pc_copy().start()

    wait_from(dz.at[0 : NZ - 1], s_dz, r_dz)
    wait_from(pall.at[1 - c], s_pc, r_pc)
    acc = jnp.zeros((16, HID), F32)
    loss = jnp.zeros((16, 128), F32)
    for g in range(NZ // 2):
        left = dz[2 * g].astype(F32) + dz[2 * g + 1].astype(F32)
        loss = loss + left
        right = jnp.concatenate(
            [pall[cc, zz] for zz in (2 * g, 2 * g + 1) for cc in range(2)], axis=0
        )
        acc = acc + dot(left[:, :64].astype(BF16), right)
    out_ref[16:32, :] = acc.astype(BF16)
    loss = jnp.sum(jnp.where(iota((16, 128), 1) >= 64, loss, 0.0), axis=1, keepdims=True)
    loss_ref[...] = loss[:1, :] * (1.0 / IMAGES)

    sent(tp.at[0:3], s_tq, r_tq)
    sent(tj.at[0 : NZ - 1], s_tz, r_tz)
    sent(c1b.at[0 : NF - 1], s_c1, r_c1)
    sent(px, s_px, r_px)
    sent(sj.at[0 : NZ - 1], s_cz, r_cz)
    sent(sp.at[0 : NP - 1], s_cp, r_cp)
    sent(da.at[0 : NP - 1], s_da, r_da)
    sent(pall.at[c, 0 : NZ - 1], s_pz, r_pz)
    sent(db.at[0 : (NF - 1) * 16], s_db.at[0], r_db.at[0])
    sent(db.at[0 : (NP - NF) * 16], s_db.at[1], r_db.at[1])
    sent(dz.at[0 : NZ - 1], s_dz, r_dz)
    sent(sib, s_co, r_co.at[0])
    sent(xs, s_x, r_x.at[0])
    sent(pall.at[c], s_pc, r_pc)

    wait_from(zb.at[0 : NW - 1], s_z, r_z)
    out_ref[0:16, :] = (totf[w] + jnp.sum(zb[...].astype(F32), axis=0)).astype(BF16)
    sent(zb.at[0 : NW - 1], s_z, r_z)


def body(tokens, teacher, norm_gain, w_in, b_in, w_out, b_out, final_gain):
    vmem = pl.BlockSpec(memory_space=pltpu.VMEM)
    one, two, four = (
        pltpu.SemaphoreType.DMA, pltpu.SemaphoreType.DMA((2,)), pltpu.SemaphoreType.DMA((4,))
    )
    sems = [one, one] * 7 + [two, two] + [one, one] * 3 + [one, four] + [one, two] + [one, one]
    packed, loss = pl.pallas_call(
        kernel,
        name="gram_step",
        out_shape=(
            jax.ShapeDtypeStruct((32, HID), BF16),
            jax.ShapeDtypeStruct((1, 1), F32),
        ),
        in_specs=[pl.BlockSpec(memory_space=pl.ANY)] * 8,
        out_specs=(vmem, vmem),
        scratch_shapes=[
            pltpu.VMEM((1024, D), BF16),
            pltpu.VMEM((8, DT), BF16),
            pltpu.VMEM((1, D), F32),
            pltpu.VMEM((D, HID), BF16),
            pltpu.VMEM((1, HID), F32),
            pltpu.VMEM((D, HID), BF16),
            pltpu.VMEM((8, 128), F32),
            pltpu.VMEM((8, 128), F32),
            pltpu.SemaphoreType.DMA((11,)),
            pltpu.VMEM((1024, D), BF16),
            pltpu.VMEM((1024, HID), F32),
            pltpu.VMEM((1024, HID), F32),
            pltpu.VMEM((1024, HID), BF16),
            pltpu.VMEM((8, D), F32),
            pltpu.VMEM((8, HID), F32),
            pltpu.VMEM((64, 128), F32),
            pltpu.VMEM((64, 128), F32),
            pltpu.VMEM((3, 128, 128), F32),
            pltpu.VMEM((4, 128, 384), BF16),
            pltpu.VMEM((NZ, 16, 384), BF16),
            pltpu.VMEM((16, 384), BF16),
            pltpu.VMEM((NF, 8, 128), F32),
            pltpu.VMEM((8, 128), F32),
            pltpu.VMEM((NP, 8, 128), F32),
            pltpu.VMEM((NZ, 8, 128), F32),
            pltpu.VMEM((NP, 8, 128), F32),
            pltpu.VMEM((NP, 8, 128), F32),
            pltpu.VMEM((16, 128), F32),
            pltpu.VMEM((NP * 16, 128), F32),
            pltpu.VMEM((8, HID), F32),
            pltpu.VMEM((8, HID), F32),
            pltpu.VMEM((16, HID), BF16),
            pltpu.VMEM((2, NZ, 16, HID), BF16),
            pltpu.VMEM((NZ, 16, 128), BF16),
            pltpu.VMEM((NZ, 16, 128), BF16),
            pltpu.VMEM((4, 2, 4, 16, HID), F32),
            pltpu.VMEM((4, 2, 4, 16, HID), BF16),
            pltpu.VMEM((4, 2, 4, 16, HID), BF16),
            pltpu.VMEM((3, 2, 4, 16, HID), BF16),
            pltpu.VMEM((2, 3, 4, 16, HID), BF16),
            pltpu.VMEM((NW, 16, HID), F32),
            pltpu.VMEM((NW, 16, HID), BF16),
            pltpu.VMEM((NW, 16, HID), BF16),
        ]
        + sems,
        compiler_params=pltpu.CompilerParams(
            collective_id=0, has_side_effects=True, vmem_limit_bytes=56 << 20
        ),
        cost_estimate=pl.CostEstimate(
            flops=5_000_000_000, bytes_accessed=8_000_000, transcendentals=1_000_000
        ),
    )(
        tokens,
        teacher,
        norm_gain.reshape(1, D),
        w_in,
        b_in.reshape(1, HID),
        w_out,
        b_out.reshape(8, 128),
        final_gain.reshape(8, 128),
    )
    return loss.reshape(()), packed[:16], packed[16:]


def solution(mesh):
    return jax.shard_map(
        body,
        mesh=mesh,
        in_specs=(
            P("dp", None),
            P("dp", None),
            P(),
            P(None, "fsdp"),
            P("fsdp"),
            P(None, "fsdp"),
            P(),
            P(),
        ),
        out_specs=(P(), P("dp", "fsdp"), P("dp", "fsdp")),
        check_vma=False,
    )
```

time: 84.6 us -> 68.5 us (0.81)
  the two profiles are of different devices: /device:TPU:33 before, /device:TPU:1 now
where the time goes in v2:
time: 68.5 us; the launch traced here: 67.9 us
  Pallas kernels  64.1 us (94%)
  between operations  2.38 us (3%)
  local copies, waits for them, and re-layouts  1.35 us (2%)
    pallas_call x1, Pallas kernels, body(): pl.pallas_call(kernel, name='gram_step', out_shape=(jax.ShapeDtypeStruct(...  64.1 us

profile of v2, /device:TPU:1, one launch (start us, length us, event | category | flops | bytes accessed | tf_op | source)
XLA Modules:
  0.0 67.9 jit_solution(4338643349001989303)
XLA Ops:
  0.6 64.1 %gram_step.1 = (bf16[32,512]{1,0:T(8,128)(2,1)}, f32[1,1]{1,0:T(1,128)}) custom-call(bf16[1024,1024]{1,0:T(8,128)(2,1)} %tok_h.1, bf16[8,6144]{1,0:T(8,128)(2,1)} %tea_h.1, f32[1,1024]{1,0:T(1,128)} %bitcast.5, bf16[1024,512]{1,0:T(8,128)(2,1)} %win_h.1, f32[1,512]{1,0:T(1,128)} %bitcast.8, bf16[1024,512]{1,0:T(8,128)(2,1)} %wout_h.1, f32[8,128]{1,0:T(8,128)} %bitcast.6, ...), custom_call_target="tpu_custom_call" | custom-call | flops 5000000000 | bytes 8000000 | tf_op jit(solution)/shard_map/gram_step/pallas_call | solution.py:479
  64.8 1.3 %fusion = (bf16[16,512]{1,0:T(8,128)(2,1)}, bf16[16,512]{1,0:T(8,128)(2,1)}) fusion(bf16[32,512]{1,0:T(8,128)(2,1)} %get-tuple-element.6), kind=kLoop, calls=%fused_computation | loop fusion | bytes 65536 | tf_op jit(solution)/shard_map/slice | solution.py:550

commit v3 on v2

--- a/solution.py
+++ b/solution.py
@@ -60,15 +60,15 @@
 
 def kernel(
     tok_h, tea_h, ng_h, win_h, b_in_h, wout_h, b_out_h, fg_h,
-    out_ref, loss_ref,
+    loss_ref, gin_ref, gout_ref,
     tok, tea, ng, win, b_in, wout, b_out, fg, s_in,
-    normed, pre, slope, dhid, tmean, pooled_f, part64, tm64,
+    normed, normed_t, pre, slope, dhid, tmean, pooled_f, part64, tm64,
     tflat, tp, tj, trow, c1b, st_row, sp, sj, dref, da, dmsg, db,
     px, pin, pout16, pall, zmsg, dz,
-    own, sib, coreb, xs, xb, totf, zs, zb,
+    own, sib, coreb, xs, xb, xm, xn, totf, zs, zb,
     s_tq, r_tq, s_tz, r_tz, s_c1, r_c1, s_px, r_px, s_cz, r_cz, s_cp, r_cp,
     s_da, r_da, s_db, r_db, s_pz, r_pz, s_pc, r_pc, s_dz, r_dz,
-    s_co, r_co, s_x, r_x, s_z, r_z,
+    s_co, r_co, s_x, r_x, s_xm, r_xm, s_z, r_z,
 ):
     d = lax.axis_index("dp")
     f = lax.axis_index("fsdp")
@@ -97,6 +97,13 @@
             return carry
 
         lax.fori_loop(lo, hi, step, 0)
+
+    def along_z(fn):
+        def step(m, carry):
+            fn(NZ // 2 + div(m + 1, 2) * (1 - 2 * rem(m, 2)))
+            return carry
+
+        lax.fori_loop(0, NZ - 1, step, 0)
 
     def load(n, src, dst):
         return pltpu.make_async_copy(src, dst, s_in.at[n])
@@ -136,8 +143,10 @@
             barrier, inc=1, device_id=dev(xl, rem(z + k, NZ), c, f), device_id_type=MESH
         )
 
-    each(1, NP, sig_plane)
-    each(1, NZ, sig_z)
+    for m in range(NZ - 1):
+        sig_z(NZ // 2 + (m + 1) // 2 * (1 - 2 * (m % 2)))
+    for k in range(1, NP):
+        sig_plane(k)
 
     loads[0].wait()
     teacher = tea[...].astype(F32)
@@ -158,25 +167,32 @@
     gain = ng[...]
     bias = b_in[...]
 
-    def forward(i):
-        load_tok(i).wait()
-        rows = pl.ds(pl.multiple_of(i * 256, 256), 256)
+    def normalise(i):
+        rows = slice(256 * i, 256 * i + 256)
         x = tok[rows, :].astype(F32)
-        tmean[pl.ds(2 * i, 1), :] = jnp.sum(x[:128], axis=0, keepdims=True) * (1.0 / PER_IMAGE)
-        tmean[pl.ds(2 * i + 1, 1), :] = jnp.sum(x[128:], axis=0, keepdims=True) * (1.0 / PER_IMAGE)
+        for n in range(2):
+            tmean[2 * i + n : 2 * i + n + 1, :] = jnp.sum(
+                x[128 * n : 128 * n + 128], axis=0, keepdims=True
+            ) * (1.0 / PER_IMAGE)
         centered = x - jnp.mean(x, axis=-1, keepdims=True)
         inv = lax.rsqrt(jnp.mean(centered * centered, axis=-1, keepdims=True) + 1e-05)
-        nb = (centered * inv * gain).astype(BF16)
-        normed[rows, :] = nb
-        act = dot(nb, win[...]) + bias
+        normed[rows, :] = (centered * inv * gain).astype(BF16)
+
+    def activate(i):
+        rows = slice(256 * i, 256 * i + 256)
+        act = dot(normed[rows, :], win[...]) + bias
         pre[rows, :] = act
         g = 0.5 * act * (1.0 + gelu_parts(act))
-        pooled_f[pl.ds(2 * i, 1), :] = jnp.sum(g[:128], axis=0, keepdims=True) * (1.0 / PER_IMAGE)
-        pooled_f[pl.ds(2 * i + 1, 1), :] = jnp.sum(g[128:], axis=0, keepdims=True) * (
-            1.0 / PER_IMAGE
-        )
-
-    each(0, 2, forward)
+        for n in range(2):
+            pooled_f[2 * i + n : 2 * i + n + 1, :] = jnp.sum(
+                g[128 * n : 128 * n + 128], axis=0, keepdims=True
+            ) * (1.0 / PER_IMAGE)
+
+    load_tok(0).wait()
+    normalise(0)
+    load_tok(1).wait()
+    activate(0)
+    normalise(1)
     pl.semaphore_wait(barrier, NP - 1 + NZ - 1)
     def tq_copy(k):
         qq = rem(q + k, 4)
@@ -187,9 +203,14 @@
     def tz_copy(k):
         return copy(trow, tj.at[z], s_tz, r_tz, dev(xl, rem(z + k, NZ), c, f))
 
-    each(1, NZ, lambda k: tz_copy(k).start())
-    each(1, 4, lambda k: tq_copy(k).start())
-    each(2, 4, forward)
+    along_z(lambda k: tz_copy(k).start())
+    load_tok(2).wait()
+    activate(1)
+    normalise(2)
+    load_tok(3).wait()
+    activate(2)
+    normalise(3)
+    activate(3)
     for item in loads[4:]:
         item.wait()
     pooled_b = pooled_f[...].astype(BF16)
@@ -214,6 +235,7 @@
         return copy(px, pin, s_px, r_px, dev(1 - xl, z, c, f))
 
     px_copy().start()
+    each(1, 4, lambda k: tq_copy(k).start())
 
     def slopes(i):
         rows = pl.ds(pl.multiple_of(i * 128, 128), 128)
@@ -254,7 +276,7 @@
         qq, ff, _ = plane(k)
         return copy(st_row, sp.at[p], s_cp, r_cp, dev(div(qq, 2), z, rem(qq, 2), ff))
 
-    each(1, NZ, lambda k: cz_copy(k).start())
+    along_z(lambda k: cz_copy(k).start())
     each(1, NP, lambda k: cp_copy(k).start())
     sj[z] = student
     sp[p] = student
@@ -280,6 +302,10 @@
     ).astype(BF16)
     pout16[...] = block16
     pall[c, z] = block16
+
+    for i in range(4):
+        turned_cols = slice(256 * i, 256 * i + 256)
+        normed_t[turned_cols, :] = normed[:, turned_cols].T
 
     wait_from(sp.at[0 : NP - 1], s_cp, r_cp)
     wait_from(sj.at[0 : NZ - 1], s_cz, r_cz)
@@ -301,7 +327,7 @@
 
     each(1, NP, lambda k: da_copy(k).start())
     da[p] = dref[p]
-    each(1, NZ, lambda k: pz_copy(k).start())
+    along_z(lambda k: pz_copy(k).start())
 
     wait_from(da.at[0 : NP - 1], s_da, r_da)
     dstudent = (LOSS_SCALE * 4.0 / IMAGES) * jnp.sum(da[...], axis=0)
@@ -344,30 +370,73 @@
     s_bit = rem(z, 2)
     w = div(z, 2)
 
+    def half(h):
+        return rem(div(w, 4) + 1 + h, 2)
+
     def co_copy(j):
         return copy(sib.at[j], coreb.at[j], s_co, r_co.at[j], dev(xl, z, 1 - c, f))
 
+    step = 1 - 2 * s_bit
+
     def near_copy(t, h):
-        xx = xl if t == 2 else 1 - xl
-        zz = 2 * w + (s_bit if t == 1 else 1 - s_bit)
-        return copy(
-            xs.at[t, h], xb.at[h, t], s_x, r_x.at[h], dev(xx, zz, c, f)
-        )
+        xx = xl if t >= 3 else 1 - xl
+        zz = z if t == 2 else rem(z + NZ + (step if t in (0, 3) else -step), NZ)
+        if t == 2:
+            return copy(xm.at[h], xn.at[h], s_xm, r_xm.at[h], dev(xx, zz, c, f))
+        n = t if t < 2 else t - 1
+        return copy(xs.at[n, h], xb.at[h, n], s_x, r_x.at[h], dev(xx, zz, c, f))
 
     def core_sum(j, bit):
         return own[j, bit] + coreb[j, bit].astype(F32)
 
     def near_send(j):
         wait_from(coreb.at[j], s_co, r_co.at[j])
-        h = j % 2
-        for t in (0, 1) if j < 2 else (2,):
-            xs[t, h] = core_sum(j, s_bit if t == 1 else 1 - s_bit).astype(BF16)
-            near_copy(t, h).start()
+        h = half(j % 2)
+        across = core_sum(j, 1 - s_bit).astype(BF16)
+        first = 0 if j < 2 else 2
+        for n in range(2):
+            xs[first + n, h] = across[:, :, 256 * n : 256 * n + 256]
+        if j < 2:
+            near_copy(0, h).start()
+            near_copy(1, h).start()
+            xm[h] = core_sum(j, s_bit).astype(BF16)
+            near_copy(2, h).start()
+        else:
+            near_copy(3, h).start()
+            near_copy(4, h).start()
+
+    def dz_copy(k):
+        zz = rem(z + k, NZ)
+        return copy(zmsg.at[zz], dz.at[z], s_dz, r_dz, dev(xl, zz, c, f))
+
+    def turn():
+        wait_from(db.at[0 : (NP - NF) * 16], s_db.at[1], r_db.at[1])
+        loss_plane = jnp.zeros((8, 128), F32)
+        for pp in range(NP):
+            loss_plane = loss_plane + db[pp * 16 + 8 : pp * 16 + 16, :]
+        flat = jnp.concatenate(
+            [db[pl.ds(xl * 4 + a, NP, stride=16), :] for a in range(4)], axis=1
+        ).astype(BF16)
+        image = iota((NP, 128), 0)
+        odd = rem(z, 2)
+        lane = odd * 32 + ((image // 8) % 2) * 16 + (image // 16) * 8 + image % 8
+        place = (lane == iota((NP, 128), 1)).astype(BF16)
+        turned = dot_first(flat, place).reshape(NZ, 2, 16, 128)
+        turned = jnp.where(low, turned[:, 0], turned[:, 1])
+        part = loss_plane[0:1, :]
+        high = part.astype(BF16).astype(F32)
+        mid = (part - high).astype(BF16).astype(F32)
+        last = part - high - mid
+        at = iota((1, 128), 1) - (64 + 4 * odd)
+        extra = jnp.where(at == 0, high, jnp.where(at == 1, mid, jnp.where(at == 2, last, 0.0)))
+        zmsg[...] = (turned + extra[None]).astype(BF16)
+        dz[z] = zmsg[z]
+        along_z(lambda k: dz_copy(k).start())
 
     for j in range(4):
         side = (1 - xl) if j < 2 else xl
-        cols = pl.ds(pl.multiple_of(side * 512 + (j % 2) * 256, 256), 256)
-        term = dot_first(normed[:, cols], dhid[...]).reshape(4, 2, 2, 16, HID)
+        cols = pl.ds(pl.multiple_of(side * 512 + half(j % 2) * 256, 256), 256)
+        term = dot(normed_t[cols, :], dhid[...]).reshape(4, 2, 2, 16, HID)
         for bit in range(2):
             mine_t, other_t = term[:, bit, 0], term[:, bit, 1]
             own[j, bit] = jnp.where(low, mine_t, other_t)
@@ -375,34 +444,8 @@
         co_copy(j).start()
         if j >= 1:
             near_send(j - 1)
-
-    wait_from(db.at[0 : (NP - NF) * 16], s_db.at[1], r_db.at[1])
-    loss_plane = jnp.zeros((8, 128), F32)
-    for pp in range(NP):
-        loss_plane = loss_plane + db[pp * 16 + 8 : pp * 16 + 16, :]
-    flat = jnp.concatenate(
-        [db[pl.ds(xl * 4 + a, NP, stride=16), :] for a in range(4)], axis=1
-    ).astype(BF16)
-    image = iota((NP, 128), 0)
-    odd = rem(z, 2)
-    lane = odd * 32 + ((image // 8) % 2) * 16 + (image // 16) * 8 + image % 8
-    place = (lane == iota((NP, 128), 1)).astype(BF16)
-    turned = dot_first(flat, place).reshape(NZ, 2, 16, 128)
-    turned = jnp.where(low, turned[:, 0], turned[:, 1])
-    part = loss_plane[0:1, :]
-    high = part.astype(BF16).astype(F32)
-    mid = (part - high).astype(BF16).astype(F32)
-    last = part - high - mid
-    at = iota((1, 128), 1) - (64 + 4 * odd)
-    extra = jnp.where(at == 0, high, jnp.where(at == 1, mid, jnp.where(at == 2, last, 0.0)))
-    zmsg[...] = (turned + extra[None]).astype(BF16)
-    dz[z] = zmsg[z]
-
-    def dz_copy(k):
-        zz = rem(z + k, NZ)
-        return copy(zmsg.at[zz], dz.at[z], s_dz, r_dz, dev(xl, zz, c, f))
-
-    each(1, NZ, lambda k: dz_copy(k).start())
+        if j == 2:
+            turn()
 
     near_send(3)
 
@@ -410,23 +453,23 @@
         ww = rem(w + k, NW)
         return copy(zs.at[ww], zb.at[w], s_z, r_z, dev(xl, 2 * ww + s_bit, c, f))
 
-    def z_start(k):
-        z_copy(k).start()
-
     zb[w] = jnp.zeros((16, HID), BF16)
     for h in range(2):
         merged = core_sum(2 + h, s_bit)
-        wait_from(xb.at[h], s_x, r_x.at[h])
-        for t in range(3):
-            merged = merged + xb[h, t].astype(F32)
-        totf[4 * h : 4 * h + 4] = merged
-        zs[4 * h : 4 * h + 4] = merged.astype(BF16)
-        for ww in range(4 * h, 4 * h + 4):
-            k = rem(ww + NW - w, NW)
-
-            @pl.when(k != 0)
+        hh = half(h)
+        wait_from(xn.at[hh], s_xm, r_xm.at[hh])
+        merged = merged + xn[hh].astype(F32)
+        wait_from(xb.at[hh], s_x, r_x.at[hh])
+        sides = [xb[hh, n].astype(F32) + xb[hh, 2 + n].astype(F32) for n in range(2)]
+        merged = merged + jnp.concatenate(sides, axis=2)
+        blocks = pl.ds(hh * 4, 4)
+        totf[blocks] = merged
+        zs[blocks] = merged.astype(BF16)
+        for k in (4, 3, 5, 2, 6, 1, 7):
+
+            @pl.when(div(rem(w + k, NW), 4) == hh)
             def _():
-                z_start(k)
+                z_copy(k).start()
 
     wait_from(pall.at[c, 0 : NZ - 1], s_pz, r_pz)
 
@@ -446,9 +489,9 @@
             [pall[cc, zz] for zz in (2 * g, 2 * g + 1) for cc in range(2)], axis=0
         )
         acc = acc + dot(left[:, :64].astype(BF16), right)
-    out_ref[16:32, :] = acc.astype(BF16)
+    gout_ref[...] = acc.astype(BF16)
     loss = jnp.sum(jnp.where(iota((16, 128), 1) >= 64, loss, 0.0), axis=1, keepdims=True)
-    loss_ref[...] = loss[:1, :] * (1.0 / IMAGES)
+    loss_ref[...] = jnp.broadcast_to(loss[:8], (8, 128)) * (1.0 / IMAGES)
 
     sent(tp.at[0:3], s_tq, r_tq)
     sent(tj.at[0 : NZ - 1], s_tz, r_tz)
@@ -463,10 +506,11 @@
     sent(dz.at[0 : NZ - 1], s_dz, r_dz)
     sent(sib, s_co, r_co.at[0])
     sent(xs, s_x, r_x.at[0])
+    sent(xm, s_xm, r_xm.at[0])
     sent(pall.at[c], s_pc, r_pc)
 
     wait_from(zb.at[0 : NW - 1], s_z, r_z)
-    out_ref[0:16, :] = (totf[w] + jnp.sum(zb[...].astype(F32), axis=0)).astype(BF16)
+    gin_ref[...] = (totf[w] + jnp.sum(zb[...].astype(F32), axis=0)).astype(BF16)
     sent(zb.at[0 : NW - 1], s_z, r_z)
 
 
@@ -475,16 +519,17 @@
     one, two, four = (
         pltpu.SemaphoreType.DMA, pltpu.SemaphoreType.DMA((2,)), pltpu.SemaphoreType.DMA((4,))
     )
-    sems = [one, one] * 7 + [two, two] + [one, one] * 3 + [one, four] + [one, two] + [one, one]
-    packed, loss = pl.pallas_call(
+    sems = [one, one] * 7 + [two, two] + [one, one] * 3 + [one, four] + [one, two] * 2 + [one, one]
+    loss, grad_in, grad_out = pl.pallas_call(
         kernel,
         name="gram_step",
         out_shape=(
-            jax.ShapeDtypeStruct((32, HID), BF16),
-            jax.ShapeDtypeStruct((1, 1), F32),
+            jax.ShapeDtypeStruct((8, 128), F32),
+            jax.ShapeDtypeStruct((16, HID), BF16),
+            jax.ShapeDtypeStruct((16, HID), BF16),
         ),
         in_specs=[pl.BlockSpec(memory_space=pl.ANY)] * 8,
-        out_specs=(vmem, vmem),
+        out_specs=(vmem, vmem, vmem),
         scratch_shapes=[
             pltpu.VMEM((1024, D), BF16),
             pltpu.VMEM((8, DT), BF16),
@@ -496,6 +541,7 @@
             pltpu.VMEM((8, 128), F32),
             pltpu.SemaphoreType.DMA((11,)),
             pltpu.VMEM((1024, D), BF16),
+            pltpu.VMEM((D, 1024), BF16),
             pltpu.VMEM((1024, HID), F32),
             pltpu.VMEM((1024, HID), F32),
             pltpu.VMEM((1024, HID), BF16),
@@ -524,8 +570,10 @@
             pltpu.VMEM((4, 2, 4, 16, HID), F32),
             pltpu.VMEM((4, 2, 4, 16, HID), BF16),
             pltpu.VMEM((4, 2, 4, 16, HID), BF16),
-            pltpu.VMEM((3, 2, 4, 16, HID), BF16),
-            pltpu.VMEM((2, 3, 4, 16, HID), BF16),
+            pltpu.VMEM((4, 2, 4, 16, HID // 2), BF16),
+            pltpu.VMEM((2, 4, 4, 16, HID // 2), BF16),
+            pltpu.VMEM((2, 4, 16, HID), BF16),
+            pltpu.VMEM((2, 4, 16, HID), BF16),
             pltpu.VMEM((NW, 16, HID), F32),
             pltpu.VMEM((NW, 16, HID), BF16),
             pltpu.VMEM((NW, 16, HID), BF16),
@@ -547,7 +595,7 @@
         b_out.reshape(8, 128),
         final_gain.reshape(8, 128),
     )
-    return loss.reshape(()), packed[:16], packed[16:]
+    return loss[0, 0], grad_in, grad_out
 
 
 def solution(mesh):

time: 68.5 us -> 67.7 us (0.988)
  local copies, waits for them, and re-layouts: 1.35 us -> 3.84 us
  between operations: 2.38 us -> 0.64 us
  Pallas kernels: 64.1 us -> 62.8 us
    unnamed x0 -> x2, local copies, waits for them, and re-layouts: none -> 2.65 us
    pallas_call x1, Pallas kernels: 64.1 us -> 62.8 us  [body(): pl.pallas_call(kernel, name='gram_step', out_shape=(jax.ShapeDtypeStruct(...]
where the time goes in v3:
time: 67.7 us; the launch traced here: 67.3 us
  Pallas kernels  62.8 us (93%)
  local copies, waits for them, and re-layouts  3.84 us (6%)
    pallas_call x1, Pallas kernels, body(): pl.pallas_call(kernel, name='gram_step', out_shape=(jax.ShapeDtypeStruct(...  62.8 us
    unnamed x2, local copies, waits for them, and re-layouts  2.65 us

profile of v3, /device:TPU:1, one launch (start us, length us, event | category | flops | bytes accessed | tf_op | source)
XLA Modules:
  0.0 67.3 jit_solution(18235495506891357915)
XLA Ops:
  0.6 62.8 %gram_step.1 = (f32[8,128]{1,0:T(8,128)}, bf16[16,512]{1,0:T(8,128)(2,1)}, bf16[16,512]{1,0:T(8,128)(2,1)}) custom-call(bf16[1024,1024]{1,0:T(8,128)(2,1)} %tok_h.1, bf16[8,6144]{1,0:T(8,128)(2,1)} %tea_h.1, f32[1,1024]{1,0:T(1,128)} %bitcast.5, bf16[1024,512]{1,0:T(8,128)(2,1)} %win_h.1, f32[1,512]{1,0:T(1,128)} %bitcast.8, bf16[1024,512]{1,0:T(8,128)(2,1)} %wout_h.1, ...), custom_call_target="tpu_custom_call" | custom-call | flops 5000000000 | bytes 8000000 | tf_op jit(solution)/shard_map/gram_step/pallas_call | solution.py:523
  63.5 1.2 %slice.3 = f32[1,1]{1,0:T(1,128)} slice(f32[8,128]{1,0:T(8,128)} %get-tuple-element.6), slice={[0:1], [0:1]} | slice | bytes 8 | tf_op jit(solution)/shard_map/slice | solution.py:598
  64.7 1.3 %copy.13 = bf16[16,512]{1,0:T(8,128)(2,1)} copy(bf16[16,512]{1,0:T(8,128)(2,1)} %get-tuple-element.13) | data formatting | bytes 32768
  66.0 1.3 %copy.14 = bf16[16,512]{1,0:T(8,128)(2,1)} copy(bf16[16,512]{1,0:T(8,128)(2,1)} %get-tuple-element.14) | data formatting | bytes 32768

commit v4 on v3

--- a/solution.py
+++ b/solution.py
@@ -60,14 +60,14 @@
 
 def kernel(
     tok_h, tea_h, ng_h, win_h, b_in_h, wout_h, b_out_h, fg_h,
-    loss_ref, gin_ref, gout_ref,
+    out_ref, loss_ref,
     tok, tea, ng, win, b_in, wout, b_out, fg, s_in,
     normed, normed_t, pre, slope, dhid, tmean, pooled_f, part64, tm64,
-    tflat, tp, tj, trow, c1b, st_row, sp, sj, dref, da, dmsg, db,
-    px, pin, pout16, pall, zmsg, dz,
+    tflat, tp, tj, trow, c1b, st_row, sp, sj, dref, da, dmsg, db, dbf,
+    px, pin, pout16, pall, zmsg, dzr, dzm, dzf,
     own, sib, coreb, xs, xb, xm, xn, totf, zs, zb,
     s_tq, r_tq, s_tz, r_tz, s_c1, r_c1, s_px, r_px, s_cz, r_cz, s_cp, r_cp,
-    s_da, r_da, s_db, r_db, s_pz, r_pz, s_pc, r_pc, s_dz, r_dz,
+    s_da, r_da, s_db, r_db, s_pz, r_pz, s_pc, r_pc, s_dz, r_dz, s_df, r_df,
     s_co, r_co, s_x, r_x, s_xm, r_xm, s_z, r_z,
 ):
     d = lax.axis_index("dp")
@@ -81,10 +81,13 @@
     def dev(xx, zz, cc, ff):
         return ((xx * NZ + zz) * 2 + cc, ff)
 
-    def plane(k):
-        qq = rem(q + div(k, NF), 4)
-        ff = rem(f + rem(k, NF), NF)
-        return qq, ff, qq * NF + ff
+    qs = [rem(q + k, 4) for k in range(4)]
+    fs = [rem(f + k, NF) for k in range(NF)]
+    ds = [(div(v, 2) * NZ + z) * 2 + rem(v, 2) for v in qs]
+    near = [(0, kf) for kf in (3, 5, 4, 7, 1, 6, 2)]
+    others = [(kq, kf) for kq in (2, 3, 1) for kf in (3, 5, 4, 7, 1, 6, 2, 0)]
+    plane = near + others
+    far_z = [NZ // 2 + (m + 1) // 2 * (1 - 2 * (m % 2)) for m in range(NZ - 1)]
 
     def copy(src, dst, ss, rs, to):
         return pltpu.make_async_remote_copy(
@@ -99,11 +102,8 @@
         lax.fori_loop(lo, hi, step, 0)
 
     def along_z(fn):
-        def step(m, carry):
-            fn(NZ // 2 + div(m + 1, 2) * (1 - 2 * rem(m, 2)))
-            return carry
-
-        lax.fori_loop(0, NZ - 1, step, 0)
+        for k in far_z:
+            fn(k)
 
     def load(n, src, dst):
         return pltpu.make_async_copy(src, dst, s_in.at[n])
@@ -132,21 +132,12 @@
 
     barrier = pltpu.get_barrier_semaphore()
 
-    def sig_plane(k):
-        qq, ff, _ = plane(k)
-        pl.semaphore_signal(
-            barrier, inc=1, device_id=dev(div(qq, 2), z, rem(qq, 2), ff), device_id_type=MESH
-        )
-
-    def sig_z(k):
+    for k in far_z:
         pl.semaphore_signal(
             barrier, inc=1, device_id=dev(xl, rem(z + k, NZ), c, f), device_id_type=MESH
         )
-
-    for m in range(NZ - 1):
-        sig_z(NZ // 2 + (m + 1) // 2 * (1 - 2 * (m % 2)))
-    for k in range(1, NP):
-        sig_plane(k)
+    for kq, kf in plane:
+        pl.semaphore_signal(barrier, inc=1, device_id=(ds[kq], fs[kf]), device_id_type=MESH)
 
     loads[0].wait()
     teacher = tea[...].astype(F32)
@@ -190,23 +181,10 @@
 
     load_tok(0).wait()
     normalise(0)
-    load_tok(1).wait()
-    activate(0)
-    normalise(1)
-    pl.semaphore_wait(barrier, NP - 1 + NZ - 1)
-    def tq_copy(k):
-        qq = rem(q + k, 4)
-        return copy(
-            tp.at[q], tp.at[q], s_tq, r_tq, dev(div(qq, 2), z, rem(qq, 2), f)
-        )
-
-    def tz_copy(k):
-        return copy(trow, tj.at[z], s_tz, r_tz, dev(xl, rem(z + k, NZ), c, f))
-
-    along_z(lambda k: tz_copy(k).start())
-    load_tok(2).wait()
-    activate(1)
-    normalise(2)
+    for i in range(2):
+        load_tok(i + 1).wait()
+        activate(i)
+        normalise(i + 1)
     load_tok(3).wait()
     activate(2)
     normalise(3)
@@ -227,7 +205,18 @@
             c1b.at[f], s_c1, r_c1, (d, ff),
         )
 
+    pl.semaphore_wait(barrier, NP - 1 + NZ - 1)
+    def tq_copy(k):
+        qq = rem(q + k, 4)
+        return copy(
+            tp.at[q], tp.at[q], s_tq, r_tq, dev(div(qq, 2), z, rem(qq, 2), f)
+        )
+
+    def tz_copy(k):
+        return copy(trow, tj.at[z], s_tz, r_tz, dev(xl, rem(z + k, NZ), c, f))
+
     each(1, NF, lambda k: c1_copy(k).start())
+    along_z(lambda k: tz_copy(k).start())
     c1b[f] = part64[pl.ds(pl.multiple_of(f * 8, 8), 8), :]
     px[...] = pooled_b.astype(F32)
 
@@ -273,11 +262,11 @@
         return copy(st_row, sj.at[z], s_cz, r_cz, dev(xl, rem(z + k, NZ), c, f))
 
     def cp_copy(k):
-        qq, ff, _ = plane(k)
-        return copy(st_row, sp.at[p], s_cp, r_cp, dev(div(qq, 2), z, rem(qq, 2), ff))
+        return copy(st_row, sp.at[p], s_cp, r_cp, (ds[k[0]], fs[k[1]]))
 
     along_z(lambda k: cz_copy(k).start())
-    each(1, NP, lambda k: cp_copy(k).start())
+    for k in plane:
+        cp_copy(k).start()
     sj[z] = student
     sp[p] = student
 
@@ -322,10 +311,12 @@
     dref[...] = dot(wide, s_other).reshape(NP, 8, 128)
 
     def da_copy(k):
-        qq, ff, pp = plane(k)
-        return copy(dref.at[pp], da.at[p], s_da, r_da, dev(div(qq, 2), z, rem(qq, 2), ff))
-
-    each(1, NP, lambda k: da_copy(k).start())
+        return copy(
+            dref.at[qs[k[0]] * NF + fs[k[1]]], da.at[p], s_da, r_da, (ds[k[0]], fs[k[1]])
+        )
+
+    for k in plane:
+        da_copy(k).start()
     da[p] = dref[p]
     along_z(lambda k: pz_copy(k).start())
 
@@ -336,27 +327,33 @@
     dembed = inv_std * (
         gain_grad - total(gain_grad) * (1.0 / D) - n_emb * (total(gain_grad * n_emb) * (1.0 / D))
     )
-    message = jnp.concatenate(
-        [dembed.astype(BF16).astype(F32), jnp.broadcast_to(share, (8, 128))], axis=0
-    )
+    high = share.astype(BF16).astype(F32)
+    mid = (share - high).astype(BF16).astype(F32)
+    last = share - high - mid
+    row = iota((8, 128), 0)
+    terms = jnp.where(row == 0, high, jnp.where(row == 1, mid, jnp.where(row == 2, last, 0.0)))
+    message = jnp.concatenate([dembed, terms], axis=0).astype(BF16)
     dmsg[...] = message
 
     def rows16(pp):
         return pl.ds(pl.multiple_of(pp * 16, 16), 16)
 
-    def db_copy(k, near):
-        qq, ff, _ = plane(k)
+    def db_copy(k, part):
         return copy(
-            dmsg, db.at[rows16(p)], s_db.at[near], r_db.at[near], dev(div(qq, 2), z, rem(qq, 2), ff)
-        )
-
-    each(1, NF, lambda k: db_copy(k, 0).start())
-    each(NF, NP, lambda k: db_copy(k, 1).start())
+            dmsg, db.at[rows16(p)], s_db.at[part], r_db.at[part], (ds[k[0]], fs[k[1]])
+        )
+
+    for k in near:
+        db_copy(k, 0).start()
+    for k in others:
+        db_copy(k, 1).start()
     db[rows16(p), :] = message
 
     wait_from(db.at[0 : (NF - 1) * 16], s_db.at[0], r_db.at[0])
+    own_rows = pl.ds(pl.multiple_of(q * (NF * 16), NF * 16), NF * 16)
+    dbf[own_rows, :] = db[own_rows, :].astype(F32)
     block = jnp.concatenate(
-        [db[pl.ds(q * (NF * 16) + a, 8, stride=16), :] for a in range(8)], axis=1
+        [dbf[pl.ds(q * (NF * 16) + a, 8, stride=16), :] for a in range(8)], axis=1
     ).astype(BF16)
     tmean[:, :HID] = dot(block, wout[...]) * (1.0 / PER_IMAGE)
 
@@ -405,33 +402,41 @@
             near_copy(3, h).start()
             near_copy(4, h).start()
 
+    octave = div(z, NF)
+    turning = rem(z, NF) == f
+
     def dz_copy(k):
         zz = rem(z + k, NZ)
-        return copy(zmsg.at[zz], dz.at[z], s_dz, r_dz, dev(xl, zz, c, f))
+        return copy(zmsg.at[zz], dzr.at[octave], s_dz, r_dz, dev(xl, zz, c, f))
 
     def turn():
         wait_from(db.at[0 : (NP - NF) * 16], s_db.at[1], r_db.at[1])
-        loss_plane = jnp.zeros((8, 128), F32)
-        for pp in range(NP):
-            loss_plane = loss_plane + db[pp * 16 + 8 : pp * 16 + 16, :]
-        flat = jnp.concatenate(
-            [db[pl.ds(xl * 4 + a, NP, stride=16), :] for a in range(4)], axis=1
-        ).astype(BF16)
-        image = iota((NP, 128), 0)
-        odd = rem(z, 2)
-        lane = odd * 32 + ((image // 8) % 2) * 16 + (image // 16) * 8 + image % 8
-        place = (lane == iota((NP, 128), 1)).astype(BF16)
-        turned = dot_first(flat, place).reshape(NZ, 2, 16, 128)
-        turned = jnp.where(low, turned[:, 0], turned[:, 1])
-        part = loss_plane[0:1, :]
-        high = part.astype(BF16).astype(F32)
-        mid = (part - high).astype(BF16).astype(F32)
-        last = part - high - mid
-        at = iota((1, 128), 1) - (64 + 4 * odd)
-        extra = jnp.where(at == 0, high, jnp.where(at == 1, mid, jnp.where(at == 2, last, 0.0)))
-        zmsg[...] = (turned + extra[None]).astype(BF16)
-        dz[z] = zmsg[z]
-        along_z(lambda k: dz_copy(k).start())
+
+        @pl.when(turning)
+        def _():
+            dbf[...] = db[...].astype(F32)
+            loss_plane = jnp.zeros((8, 128), F32)
+            for pp in range(NP):
+                loss_plane = loss_plane + dbf[pp * 16 + 8 : pp * 16 + 16, :]
+            loss_plane = jnp.sum(loss_plane, axis=0, keepdims=True)
+            flat = jnp.concatenate(
+                [dbf[pl.ds(xl * 4 + a, NP, stride=16), :] for a in range(4)], axis=1
+            ).astype(BF16)
+            image = iota((NP, 128), 0)
+            lane = octave * 32 + ((image // 8) % 2) * 16 + (image // 16) * 8 + image % 8
+            place = (lane == iota((NP, 128), 1)).astype(BF16)
+            turned = dot_first(flat, place).reshape(NZ, 2, 16, 128)
+            turned = jnp.where(low, turned[:, 0], turned[:, 1])
+            high = loss_plane.astype(BF16).astype(F32)
+            mid = (loss_plane - high).astype(BF16).astype(F32)
+            last = loss_plane - high - mid
+            at = iota((1, 128), 1) - (64 + 4 * octave)
+            extra = jnp.where(
+                at == 0, high, jnp.where(at == 1, mid, jnp.where(at == 2, last, 0.0))
+            )
+            zmsg[...] = (turned + extra[None]).astype(BF16)
+            dzr[octave] = zmsg[z]
+            along_z(lambda k: dz_copy(k).start())
 
     for j in range(4):
         side = (1 - xl) if j < 2 else xl
@@ -471,25 +476,40 @@
             def _():
                 z_copy(k).start()
 
-    wait_from(pall.at[c, 0 : NZ - 1], s_pz, r_pz)
+    @pl.when(turning)
+    def _():
+        wait_from(dzr.at[1 - octave], s_dz, r_dz)
+
+    @pl.when(jnp.logical_not(turning))
+    def _():
+        wait_from(dzr, s_dz, r_dz)
+
+    pair = (dzr[0].astype(F32) + dzr[1].astype(F32)).astype(BF16)
+    dzm[...] = pair
+    dzf[f] = pair
+
+    def df_copy(k):
+        return copy(dzm, dzf.at[f], s_df, r_df, (d, fs[k]))
+
+    for _, kf in near:
+        df_copy(kf).start()
 
     def pc_copy():
         return copy(pall.at[c], pall.at[c], s_pc, r_pc, dev(xl, z, 1 - c, f))
 
+    wait_from(pall.at[c, 0 : NZ - 1], s_pz, r_pz)
     pc_copy().start()
 
-    wait_from(dz.at[0 : NZ - 1], s_dz, r_dz)
+    wait_from(dzf.at[0 : NF - 1], s_df, r_df)
     wait_from(pall.at[1 - c], s_pc, r_pc)
     acc = jnp.zeros((16, HID), F32)
     loss = jnp.zeros((16, 128), F32)
-    for g in range(NZ // 2):
-        left = dz[2 * g].astype(F32) + dz[2 * g + 1].astype(F32)
-        loss = loss + left
-        right = jnp.concatenate(
-            [pall[cc, zz] for zz in (2 * g, 2 * g + 1) for cc in range(2)], axis=0
-        )
-        acc = acc + dot(left[:, :64].astype(BF16), right)
-    gout_ref[...] = acc.astype(BF16)
+    for g in range(NF):
+        left = dzf[g]
+        loss = loss + left.astype(F32)
+        right = jnp.concatenate([pall[cc, zz] for zz in (g, g + NF) for cc in range(2)], axis=0)
+        acc = acc + dot(left[:, :64], right)
+    out_ref[16:32, :] = acc.astype(BF16)
     loss = jnp.sum(jnp.where(iota((16, 128), 1) >= 64, loss, 0.0), axis=1, keepdims=True)
     loss_ref[...] = jnp.broadcast_to(loss[:8], (8, 128)) * (1.0 / IMAGES)
 
@@ -503,14 +523,19 @@
     sent(pall.at[c, 0 : NZ - 1], s_pz, r_pz)
     sent(db.at[0 : (NF - 1) * 16], s_db.at[0], r_db.at[0])
     sent(db.at[0 : (NP - NF) * 16], s_db.at[1], r_db.at[1])
-    sent(dz.at[0 : NZ - 1], s_dz, r_dz)
+    sent(dzf.at[0 : NF - 1], s_df, r_df)
+
+    @pl.when(turning)
+    def _():
+        sent(zmsg.at[0 : NZ - 1], s_dz, r_dz)
+
     sent(sib, s_co, r_co.at[0])
     sent(xs, s_x, r_x.at[0])
     sent(xm, s_xm, r_xm.at[0])
     sent(pall.at[c], s_pc, r_pc)
 
     wait_from(zb.at[0 : NW - 1], s_z, r_z)
-    gin_ref[...] = (totf[w] + jnp.sum(zb[...].astype(F32), axis=0)).astype(BF16)
+    out_ref[0:16, :] = (totf[w] + jnp.sum(zb[...].astype(F32), axis=0)).astype(BF16)
     sent(zb.at[0 : NW - 1], s_z, r_z)
 
 
@@ -519,17 +544,16 @@
     one, two, four = (
         pltpu.SemaphoreType.DMA, pltpu.SemaphoreType.DMA((2,)), pltpu.SemaphoreType.DMA((4,))
     )
-    sems = [one, one] * 7 + [two, two] + [one, one] * 3 + [one, four] + [one, two] * 2 + [one, one]
-    loss, grad_in, grad_out = pl.pallas_call(
+    sems = [one, one] * 7 + [two, two] + [one, one] * 4 + [one, four] + [one, two] * 2 + [one, one]
+    packed, loss = pl.pallas_call(
         kernel,
         name="gram_step",
         out_shape=(
+            jax.ShapeDtypeStruct((32, HID), BF16),
             jax.ShapeDtypeStruct((8, 128), F32),
-            jax.ShapeDtypeStruct((16, HID), BF16),
-            jax.ShapeDtypeStruct((16, HID), BF16),
         ),
         in_specs=[pl.BlockSpec(memory_space=pl.ANY)] * 8,
-        out_specs=(vmem, vmem, vmem),
+        out_specs=(vmem, vmem),
         scratch_shapes=[
             pltpu.VMEM((1024, D), BF16),
             pltpu.VMEM((8, DT), BF16),
@@ -559,14 +583,17 @@
             pltpu.VMEM((NZ, 8, 128), F32),
             pltpu.VMEM((NP, 8, 128), F32),
             pltpu.VMEM((NP, 8, 128), F32),
-            pltpu.VMEM((16, 128), F32),
+            pltpu.VMEM((16, 128), BF16),
+            pltpu.VMEM((NP * 16, 128), BF16),
             pltpu.VMEM((NP * 16, 128), F32),
             pltpu.VMEM((8, HID), F32),
             pltpu.VMEM((8, HID), F32),
             pltpu.VMEM((16, HID), BF16),
             pltpu.VMEM((2, NZ, 16, HID), BF16),
             pltpu.VMEM((NZ, 16, 128), BF16),
-            pltpu.VMEM((NZ, 16, 128), BF16),
+            pltpu.VMEM((2, 16, 128), BF16),
+            pltpu.VMEM((16, 128), BF16),
+            pltpu.VMEM((NF, 16, 128), BF16),
             pltpu.VMEM((4, 2, 4, 16, HID), F32),
             pltpu.VMEM((4, 2, 4, 16, HID), BF16),
             pltpu.VMEM((4, 2, 4, 16, HID), BF16),
@@ -595,7 +622,7 @@
         b_out.reshape(8, 128),
         final_gain.reshape(8, 128),
     )
-    return loss[0, 0], grad_in, grad_out
+    return loss[0, 0], packed[:16], packed[16:]
 
 
 def solution(mesh):

time: 67.7 us -> 64 us (0.945)
  the two profiles are of different devices: /device:TPU:1 before, /device:TPU:32 now
where the time goes in v4:
time: 64 us; the launch traced here: 63.7 us
  Pallas kernels  60.6 us (95%)
  local copies, waits for them, and re-layouts  2.53 us (4%)
  between operations  0.64 us (1%)
    pallas_call x1, Pallas kernels, body(): pl.pallas_call(kernel, name='gram_step', out_shape=(jax.ShapeDtypeStruct(...  60.6 us
    slice x2, local copies, waits for them, and re-layouts, body(): return (loss[0, 0], packed[:16], packed[16:])  2.53 us

profile of v4, /device:TPU:32, one launch (start us, length us, event | category | flops | bytes accessed | tf_op | source)
XLA Modules:
  0.0 63.7 jit_solution(6926539284115348702)
XLA Ops:
  0.6 60.6 %gram_step.1 = (bf16[32,512]{1,0:T(8,128)(2,1)}, f32[8,128]{1,0:T(8,128)}) custom-call(bf16[1024,1024]{1,0:T(8,128)(2,1)} %tok_h.1, bf16[8,6144]{1,0:T(8,128)(2,1)} %tea_h.1, f32[1,1024]{1,0:T(1,128)} %bitcast.5, bf16[1024,512]{1,0:T(8,128)(2,1)} %win_h.1, f32[1,512]{1,0:T(1,128)} %bitcast.8, bf16[1024,512]{1,0:T(8,128)(2,1)} %wout_h.1, f32[8,128]{1,0:T(8,128)} %bitcast.6, ...), custom_call_target="tpu_custom_call" | custom-call | flops 5000000000 | bytes 8000000 | tf_op jit(solution)/shard_map/gram_step/pallas_call | solution.py:548
  61.2 1.2 %slice.9 = f32[1,1]{1,0:T(1,128)} slice(f32[8,128]{1,0:T(8,128)} %get-tuple-element.5), slice={[0:1], [0:1]} | slice | bytes 8 | tf_op jit(solution)/shard_map/slice | solution.py:625
  62.4 1.3 %fusion = (bf16[16,512]{1,0:T(8,128)(2,1)}, bf16[16,512]{1,0:T(8,128)(2,1)}) fusion(bf16[32,512]{1,0:T(8,128)(2,1)} %get-tuple-element.6), kind=kLoop, calls=%fused_computation | loop fusion | bytes 65536 | tf_op jit(solution)/shard_map/slice | solution.py:625

commit v5 on v4

--- a/solution.py
+++ b/solution.py
@@ -68,7 +68,7 @@
     own, sib, coreb, xs, xb, xm, xn, totf, zs, zb,
     s_tq, r_tq, s_tz, r_tz, s_c1, r_c1, s_px, r_px, s_cz, r_cz, s_cp, r_cp,
     s_da, r_da, s_db, r_db, s_pz, r_pz, s_pc, r_pc, s_dz, r_dz, s_df, r_df,
-    s_co, r_co, s_x, r_x, s_xm, r_xm, s_z, r_z,
+    s_co, r_co, s_x, r_x, s_xm, r_xm, s_z, r_z, s_far,
 ):
     d = lax.axis_index("dp")
     f = lax.axis_index("fsdp")
@@ -88,6 +88,9 @@
     others = [(kq, kf) for kq in (2, 3, 1) for kf in (3, 5, 4, 7, 1, 6, 2, 0)]
     plane = near + others
     far_z = [NZ // 2 + (m + 1) // 2 * (1 - 2 * (m % 2)) for m in range(NZ - 1)]
+    step_z = NZ // 4
+    close_z = [k for k in far_z if min(k, NZ - k) <= step_z]
+    away_z = [k for k in far_z if k not in close_z]
 
     def copy(src, dst, ss, rs, to):
         return pltpu.make_async_remote_copy(
@@ -101,8 +104,8 @@
 
         lax.fori_loop(lo, hi, step, 0)
 
-    def along_z(fn):
-        for k in far_z:
+    def along_z(fn, steps=far_z):
+        for k in steps:
             fn(k)
 
     def load(n, src, dst):
@@ -132,7 +135,7 @@
 
     barrier = pltpu.get_barrier_semaphore()
 
-    for k in far_z:
+    for k in close_z:
         pl.semaphore_signal(
             barrier, inc=1, device_id=dev(xl, rem(z + k, NZ), c, f), device_id_type=MESH
         )
@@ -185,6 +188,16 @@
         load_tok(i + 1).wait()
         activate(i)
         normalise(i + 1)
+    def tz_copy(k):
+        return copy(trow, tj.at[z], s_tz, r_tz, dev(xl, rem(z + k, NZ), c, f))
+
+    pl.semaphore_wait(barrier, NP - 1 + len(close_z))
+    for k in (step_z, NZ - step_z):
+        pl.semaphore_signal(
+            s_far, inc=1, device_id=dev(xl, rem(z + k, NZ), c, f), device_id_type=MESH
+        )
+    along_z(lambda k: tz_copy(k).start(), close_z)
+
     load_tok(3).wait()
     activate(2)
     normalise(3)
@@ -205,18 +218,14 @@
             c1b.at[f], s_c1, r_c1, (d, ff),
         )
 
-    pl.semaphore_wait(barrier, NP - 1 + NZ - 1)
     def tq_copy(k):
         qq = rem(q + k, 4)
         return copy(
             tp.at[q], tp.at[q], s_tq, r_tq, dev(div(qq, 2), z, rem(qq, 2), f)
         )
 
-    def tz_copy(k):
-        return copy(trow, tj.at[z], s_tz, r_tz, dev(xl, rem(z + k, NZ), c, f))
 
     each(1, NF, lambda k: c1_copy(k).start())
-    along_z(lambda k: tz_copy(k).start())
     c1b[f] = part64[pl.ds(pl.multiple_of(f * 8, 8), 8), :]
     px[...] = pooled_b.astype(F32)
 
@@ -241,6 +250,9 @@
 
     def sent(src, ss, rs):
         copy(src, src, ss, rs, (d, f)).wait_send()
+
+    pl.semaphore_wait(s_far, 2)
+    along_z(lambda k: tz_copy(k).start(), away_z)
 
     wait_from(c1b.at[0 : NF - 1], s_c1, r_c1)
     embedding = jnp.sum(c1b[...], axis=0) + tm64[pl.ds(pl.multiple_of(f * 8, 8), 8), :] + b_out[...]
@@ -270,6 +282,10 @@
     sj[z] = student
     sp[p] = student
 
+    for i in range(4):
+        turned_cols = slice(256 * i, 256 * i + 256)
+        normed_t[turned_cols, :] = normed[:, turned_cols].T
+
     wait_from(tp.at[0:3], s_tq, r_tq)
     wait_from(tj.at[0 : NZ - 1], s_tz, r_tz)
     tx = dot_last(tp[...].reshape(NP * 16, 384), tj[...].reshape(NZ * 16, 384))
@@ -291,10 +307,6 @@
     ).astype(BF16)
     pout16[...] = block16
     pall[c, z] = block16
-
-    for i in range(4):
-        turned_cols = slice(256 * i, 256 * i + 256)
-        normed_t[turned_cols, :] = normed[:, turned_cols].T
 
     wait_from(sp.at[0 : NP - 1], s_cp, r_cp)
     wait_from(sj.at[0 : NZ - 1], s_cz, r_cz)
@@ -375,32 +387,31 @@
 
     step = 1 - 2 * s_bit
 
-    def near_copy(t, h):
+    def near_copy(t, quarter):
         xx = xl if t >= 3 else 1 - xl
         zz = z if t == 2 else rem(z + NZ + (step if t in (0, 3) else -step), NZ)
+        to = dev(xx, zz, c, f)
         if t == 2:
-            return copy(xm.at[h], xn.at[h], s_xm, r_xm.at[h], dev(xx, zz, c, f))
+            return copy(xm.at[quarter], xn.at[quarter], s_xm, r_xm.at[quarter], to)
         n = t if t < 2 else t - 1
-        return copy(xs.at[n, h], xb.at[h, n], s_x, r_x.at[h], dev(xx, zz, c, f))
+        return copy(xs.at[n, quarter], xb.at[quarter, n], s_x, r_x.at[quarter], to)
 
     def core_sum(j, bit):
         return own[j, bit] + coreb[j, bit].astype(F32)
 
     def near_send(j):
         wait_from(coreb.at[j], s_co, r_co.at[j])
-        h = half(j % 2)
         across = core_sum(j, 1 - s_bit).astype(BF16)
-        first = 0 if j < 2 else 2
-        for n in range(2):
-            xs[first + n, h] = across[:, :, 256 * n : 256 * n + 256]
-        if j < 2:
-            near_copy(0, h).start()
-            near_copy(1, h).start()
-            xm[h] = core_sum(j, s_bit).astype(BF16)
-            near_copy(2, h).start()
-        else:
-            near_copy(3, h).start()
-            near_copy(4, h).start()
+        along = core_sum(j, s_bit).astype(BF16) if j < 2 else None
+        for u in range(2):
+            quarter = half(j % 2) * 2 + u
+            for n in range(2):
+                t = n if j < 2 else 3 + n
+                xs[t - t // 3, quarter] = across[2 * u : 2 * u + 2, :, 256 * n : 256 * n + 256]
+                near_copy(t, quarter).start()
+            if j < 2:
+                xm[quarter] = along[2 * u : 2 * u + 2]
+                near_copy(2, quarter).start()
 
     octave = div(z, NF)
     turning = rem(z, NF) == f
@@ -460,21 +471,24 @@
 
     zb[w] = jnp.zeros((16, HID), BF16)
     for h in range(2):
-        merged = core_sum(2 + h, s_bit)
-        hh = half(h)
-        wait_from(xn.at[hh], s_xm, r_xm.at[hh])
-        merged = merged + xn[hh].astype(F32)
-        wait_from(xb.at[hh], s_x, r_x.at[hh])
-        sides = [xb[hh, n].astype(F32) + xb[hh, 2 + n].astype(F32) for n in range(2)]
-        merged = merged + jnp.concatenate(sides, axis=2)
-        blocks = pl.ds(hh * 4, 4)
-        totf[blocks] = merged
-        zs[blocks] = merged.astype(BF16)
-        for k in (4, 3, 5, 2, 6, 1, 7):
-
-            @pl.when(div(rem(w + k, NW), 4) == hh)
-            def _():
-                z_copy(k).start()
+        kept = core_sum(2 + h, s_bit)
+        for u in range(2):
+            quarter = half(h) * 2 + u
+            wait_from(xn.at[quarter], s_xm, r_xm.at[quarter])
+            merged = kept[2 * u : 2 * u + 2] + xn[quarter].astype(F32)
+            wait_from(xb.at[quarter], s_x, r_x.at[quarter])
+            sides = [
+                xb[quarter, n].astype(F32) + xb[quarter, 2 + n].astype(F32) for n in range(2)
+            ]
+            merged = merged + jnp.concatenate(sides, axis=2)
+            blocks = pl.ds(quarter * 2, 2)
+            totf[blocks] = merged
+            zs[blocks] = merged.astype(BF16)
+            for k in (4, 3, 5, 2, 6, 1, 7):
+
+                @pl.when(div(rem(w + k, NW), 2) == quarter)
+                def _():
+                    z_copy(k).start()
 
     @pl.when(turning)
     def _():
@@ -544,7 +558,7 @@
     one, two, four = (
         pltpu.SemaphoreType.DMA, pltpu.SemaphoreType.DMA((2,)), pltpu.SemaphoreType.DMA((4,))
     )
-    sems = [one, one] * 7 + [two, two] + [one, one] * 4 + [one, four] + [one, two] * 2 + [one, one]
+    sems = [one, one] * 7 + [two, two] + [one, one] * 4 + [one, four] + [one, four] * 2 + [one, one]
     packed, loss = pl.pallas_call(
         kernel,
         name="gram_step",
@@ -597,15 +611,16 @@
             pltpu.VMEM((4, 2, 4, 16, HID), F32),
             pltpu.VMEM((4, 2, 4, 16, HID), BF16),
             pltpu.VMEM((4, 2, 4, 16, HID), BF16),
-            pltpu.VMEM((4, 2, 4, 16, HID // 2), BF16),
-            pltpu.VMEM((2, 4, 4, 16, HID // 2), BF16),
-            pltpu.VMEM((2, 4, 16, HID), BF16),
-            pltpu.VMEM((2, 4, 16, HID), BF16),
+            pltpu.VMEM((4, 4, 2, 16, HID // 2), BF16),
+            pltpu.VMEM((4, 4, 2, 16, HID // 2), BF16),
+            pltpu.VMEM((4, 2, 16, HID), BF16),
+            pltpu.VMEM((4, 2, 16, HID), BF16),
             pltpu.VMEM((NW, 16, HID), F32),
             pltpu.VMEM((NW, 16, HID), BF16),
             pltpu.VMEM((NW, 16, HID), BF16),
         ]
-        + sems,
+        + sems
+        + [pltpu.SemaphoreType.REGULAR],
         compiler_params=pltpu.CompilerParams(
             collective_id=0, has_side_effects=True, vmem_limit_bytes=56 << 20
         ),

time: 64 us -> 63.6 us (level)
  the two profiles are of different devices: /device:TPU:32 before, /device:TPU:1 now
where the time goes in v5:
time: 63.6 us; the launch traced here: 63.3 us
  Pallas kernels  60.1 us (94%)
  local copies, waits for them, and re-layouts  2.53 us (4%)
  between operations  0.64 us (1%)
    pallas_call x1, Pallas kernels, body(): pl.pallas_call(kernel, name='gram_step', out_shape=(jax.ShapeDtypeStruct(...  60.1 us
    slice x2, local copies, waits for them, and re-layouts, body(): return (loss[0, 0], packed[:16], packed[16:])  2.53 us

profile of v5, /device:TPU:1, one launch (start us, length us, event | category | flops | bytes accessed | tf_op | source)
XLA Modules:
  0.0 63.3 jit_solution(10140969633859960509)
XLA Ops:
  0.6 60.1 %gram_step.1 = (bf16[32,512]{1,0:T(8,128)(2,1)}, f32[8,128]{1,0:T(8,128)}) custom-call(bf16[1024,1024]{1,0:T(8,128)(2,1)} %tok_h.1, bf16[8,6144]{1,0:T(8,128)(2,1)} %tea_h.1, f32[1,1024]{1,0:T(1,128)} %bitcast.5, bf16[1024,512]{1,0:T(8,128)(2,1)} %win_h.1, f32[1,512]{1,0:T(1,128)} %bitcast.8, bf16[1024,512]{1,0:T(8,128)(2,1)} %wout_h.1, f32[8,128]{1,0:T(8,128)} %bitcast.6, ...), custom_call_target="tpu_custom_call" | custom-call | flops 5000000000 | bytes 8000000 | tf_op jit(solution)/shard_map/gram_step/pallas_call | solution.py:562
  60.8 1.2 %slice.9 = f32[1,1]{1,0:T(1,128)} slice(f32[8,128]{1,0:T(8,128)} %get-tuple-element.5), slice={[0:1], [0:1]} | slice | bytes 8 | tf_op jit(solution)/shard_map/slice | solution.py:640
  62.0 1.3 %fusion = (bf16[16,512]{1,0:T(8,128)(2,1)}, bf16[16,512]{1,0:T(8,128)(2,1)}) fusion(bf16[32,512]{1,0:T(8,128)(2,1)} %get-tuple-element.6), kind=kLoop, calls=%fused_computation | loop fusion | bytes 65536 | tf_op jit(solution)/shard_map/slice | solution.py:640

commit v6 on v5

--- a/solution.py
+++ b/solution.py
@@ -225,7 +225,8 @@
         )
 
 
-    each(1, NF, lambda k: c1_copy(k).start())
+    for _, kf in near:
+        c1_copy(kf).start()
     c1b[f] = part64[pl.ds(pl.multiple_of(f * 8, 8), 8), :]
     px[...] = pooled_b.astype(F32)
 
@@ -233,7 +234,6 @@
         return copy(px, pin, s_px, r_px, dev(1 - xl, z, c, f))
 
     px_copy().start()
-    each(1, 4, lambda k: tq_copy(k).start())
 
     def slopes(i):
         rows = pl.ds(pl.multiple_of(i * 128, 128), 128)
@@ -279,6 +279,7 @@
     along_z(lambda k: cz_copy(k).start())
     for k in plane:
         cp_copy(k).start()
+    each(1, 4, lambda k: tq_copy(k).start())
     sj[z] = student
     sp[p] = student
 
@@ -330,7 +331,7 @@
     for k in plane:
         da_copy(k).start()
     da[p] = dref[p]
-    along_z(lambda k: pz_copy(k).start())
+    along_z(lambda k: pz_copy(k).start(), away_z)
 
     wait_from(da.at[0 : NP - 1], s_da, r_da)
     dstudent = (LOSS_SCALE * 4.0 / IMAGES) * jnp.sum(da[...], axis=0)
@@ -359,6 +360,7 @@
         db_copy(k, 0).start()
     for k in others:
         db_copy(k, 1).start()
+    along_z(lambda k: pz_copy(k).start(), close_z)
     db[rows16(p), :] = message
 
     wait_from(db.at[0 : (NF - 1) * 16], s_db.at[0], r_db.at[0])
@@ -396,21 +398,24 @@
         n = t if t < 2 else t - 1
         return copy(xs.at[n, quarter], xb.at[quarter, n], s_x, r_x.at[quarter], to)
 
-    def core_sum(j, bit):
-        return own[j, bit] + coreb[j, bit].astype(F32)
+    def part(h, u):
+        return rem(div(rem(w, 4), 2) + h + u, 2)
+
+    def core_sum(j, bit, u):
+        two = pl.ds(2 * part(j % 2, u), 2)
+        return own[j, bit, two] + coreb[j, bit, two].astype(F32)
 
     def near_send(j):
         wait_from(coreb.at[j], s_co, r_co.at[j])
-        across = core_sum(j, 1 - s_bit).astype(BF16)
-        along = core_sum(j, s_bit).astype(BF16) if j < 2 else None
         for u in range(2):
-            quarter = half(j % 2) * 2 + u
+            quarter = half(j % 2) * 2 + part(j % 2, u)
+            across = core_sum(j, 1 - s_bit, u).astype(BF16)
             for n in range(2):
                 t = n if j < 2 else 3 + n
-                xs[t - t // 3, quarter] = across[2 * u : 2 * u + 2, :, 256 * n : 256 * n + 256]
+                xs[t - t // 3, quarter] = across[:, :, 256 * n : 256 * n + 256]
                 near_copy(t, quarter).start()
             if j < 2:
-                xm[quarter] = along[2 * u : 2 * u + 2]
+                xm[quarter] = core_sum(j, s_bit, u).astype(BF16)
                 near_copy(2, quarter).start()
 
     octave = div(z, NF)
@@ -471,11 +476,10 @@
 
     zb[w] = jnp.zeros((16, HID), BF16)
     for h in range(2):
-        kept = core_sum(2 + h, s_bit)
         for u in range(2):
-            quarter = half(h) * 2 + u
+            quarter = half(h) * 2 + part(h, u)
             wait_from(xn.at[quarter], s_xm, r_xm.at[quarter])
-            merged = kept[2 * u : 2 * u + 2] + xn[quarter].astype(F32)
+            merged = core_sum(2 + h, s_bit, u) + xn[quarter].astype(F32)
             wait_from(xb.at[quarter], s_x, r_x.at[quarter])
             sides = [
                 xb[quarter, n].astype(F32) + xb[quarter, 2 + n].astype(F32) for n in range(2)

time: 63.6 us -> 63.1 us (level)
  no operation moved by 1% of the time
where the time goes in v6:
time: 63.1 us; the launch traced here: 62.8 us
  Pallas kernels  59.7 us (95%)
  local copies, waits for them, and re-layouts  2.53 us (4%)
  between operations  0.64 us (1%)
    pallas_call x1, Pallas kernels, body(): pl.pallas_call(kernel, name='gram_step', out_shape=(jax.ShapeDtypeStruct(...  59.7 us
    slice x2, local copies, waits for them, and re-layouts, body(): return (loss[0, 0], packed[:16], packed[16:])  2.53 us

profile of v6, /device:TPU:1, one launch (start us, length us, event | category | flops | bytes accessed | tf_op | source)
XLA Modules:
  0.0 62.8 jit_solution(5970886275908493680)
XLA Ops:
  0.6 59.7 %gram_step.1 = (bf16[32,512]{1,0:T(8,128)(2,1)}, f32[8,128]{1,0:T(8,128)}) custom-call(bf16[1024,1024]{1,0:T(8,128)(2,1)} %tok_h.1, bf16[8,6144]{1,0:T(8,128)(2,1)} %tea_h.1, f32[1,1024]{1,0:T(1,128)} %bitcast.5, bf16[1024,512]{1,0:T(8,128)(2,1)} %win_h.1, f32[1,512]{1,0:T(1,128)} %bitcast.8, bf16[1024,512]{1,0:T(8,128)(2,1)} %wout_h.1, f32[8,128]{1,0:T(8,128)} %bitcast.6, ...), custom_call_target="tpu_custom_call" | custom-call | flops 5000000000 | bytes 8000000 | tf_op jit(solution)/shard_map/gram_step/pallas_call | solution.py:566
  60.3 1.2 %slice.9 = f32[1,1]{1,0:T(1,128)} slice(f32[8,128]{1,0:T(8,128)} %get-tuple-element.5), slice={[0:1], [0:1]} | slice | bytes 8 | tf_op jit(solution)/shard_map/slice | solution.py:644
  61.5 1.3 %fusion = (bf16[16,512]{1,0:T(8,128)(2,1)}, bf16[16,512]{1,0:T(8,128)(2,1)}) fusion(bf16[32,512]{1,0:T(8,128)(2,1)} %get-tuple-element.6), kind=kLoop, calls=%fused_computation | loop fusion | bytes 65536 | tf_op jit(solution)/shard_map/slice | solution.py:644
